TPU v7x, 256 devices: a whole 4x4x8 slice. The times are simulated.
256 devices in a mesh: row: 32 (over x_lo, z, core), col: 8 (over x_hi, y).
Axes of the slice: x: 4 (x_hi: 2, x_lo: 2; x = x_hi * 2 + x_lo), y: 4, z: 8, core: 2. Of those that a mesh axis runs over, the one named last changes fastest.
Arguments:
- amplitudes: float32 [4096, 8192], P(('col', 'row')), may hold values from -6 to 6
- integrals: float32 [8192, 8192], P('col', 'row'), may hold values from -0.0625 to 0.0625
- other_terms: float32 [4096, 8192], P('col', 'row'), may hold values from -6 to 6
- occupied_first: int32 [4096], P('col'), may hold values from 0 to 99
- occupied_second: int32 [4096], P('col'), may hold values from 0 to 99
- virtual_first: int32 [8192], P('row'), may hold values from 0 to 599
- virtual_second: int32 [8192], P('row'), may hold values from 0 to 599
- occupied_energy: float32 [100], replicated, may hold values from -2 to -0.5
- virtual_energy: float32 [600], replicated, may hold values from 0.2 to 2.5
Outputs:
- new_amplitudes: float32 [4096, 8192], P('col', 'row')
All inputs are finite; a program needn't handle non-finite values.
Results may differ from a plain program's by a relative error of at most 0.000068.
Values sent between devices are 32-bit elements; how exact they have to be, the bound alone decides.
A program may use at most 128 MiB of HBM per device.

v0:
```python
import jax
import jax.numpy as jnp
from jax import lax
from jax.sharding import PartitionSpec as P


def lookup(index, table):
    onehot = (index[:, None] == jnp.arange(table.shape[0], dtype=jnp.int32)[None, :]).astype(
        jnp.float32
    )
    return jnp.dot(
        onehot, table, precision=lax.Precision.HIGHEST, preferred_element_type=jnp.float32
    )


def local(
    amplitudes,
    integrals,
    other_terms,
    occupied_first,
    occupied_second,
    virtual_first,
    virtual_second,
    occupied_energy,
    virtual_energy,
):
    column_panel = lax.all_gather(integrals, "col", axis=0, tiled=True)
    occupied_sum = lookup(occupied_first, occupied_energy) + lookup(
        occupied_second, occupied_energy
    )
    virtual_sum = lookup(virtual_first, virtual_energy) + lookup(virtual_second, virtual_energy)
    denominator = virtual_sum[None, :] - occupied_sum[:, None]
    panel = lax.all_to_all(amplitudes, "row", split_axis=1, concat_axis=0, tiled=True)
    ladder = jnp.dot(
        lax.all_gather(panel, "row", axis=1, tiled=True),
        column_panel,
        precision=lax.Precision.HIGHEST,
        preferred_element_type=jnp.float32,
    )
    return panel + (other_terms + ladder) / denominator


def solution(mesh):
    in_specs = (
        P(("col", "row"), None),
        P("col", "row"),
        P("col", "row"),
        P("col"),
        P("col"),
        P("row"),
        P("row"),
        P(),
        P(),
    )
    out_specs = P("col", "row")
    return jax.shard_map(local, mesh=mesh, in_specs=in_specs, out_specs=out_specs, check_vma=False)
```

profile of v0, /device:TPU:1, one launch (start us, length us, event | category | flops | bytes accessed | tf_op | source)
XLA Modules:
  0.0 253.1 jit_solution(9382043790775873873)
XLA Ops:
  6.5 0.0 copy-start
  6.5 0.0 all-gather.5.cloned.1.call-start
  6.5 0.7 all-gather.5.cloned.1.call-update
  7.3 0.0 all-gather.3.cloned.1.call-start
  7.3 1.1 copy.13
  8.4 27.5 %all_to_all.19 = f32[16,32,256]{2,0,1:T(8,128)} all-to-all(f32[16,32,256]{2,0,1:T(8,128)S(1)} %bitcast.23), channel_id=1, replica_groups=mesh['row'=32,'col'=8] {'row'}, dimensions={1} | all-to-all | bytes 1048576 | tf_op jit(solution)/shard_map/all_to_all | solution.py:33
  35.9 0.0 all-gather.3.cloned.1.call-update
  36.0 0.7 reshape.9
  36.7 0.0 copy-done
  36.7 1.0 fusion.6
  37.6 1.0 fusion.7
  38.7 1.1 fusion.3
  39.8 1.2 fusion.2
  41.0 86.3 %all-gather.5.cloned.1.call-done = f32[8192,256]{1,0:T(8,128)} async-done(((f32[1024,256]{1,0:T(8,128)}), f32[8192,256]{1,0:T(8,128)}) %all-gather.5.cloned.1.call-update) | async-done | bytes 8388624 | tf_op jit(solution)/shard_map/all_gather | solution.py:27
  127.2 100.4 %all-gather.3.cloned.1.call-done = f32[512,8192]{1,0:T(8,128)} async-done(((f32[512,256]{1,0:T(8,128)}), f32[512,8192]{1,0:T(8,128)}) %all-gather.3.cloned.1.call-update) | async-done | bytes 16777232 | tf_op jit(solution)/shard_map/all_gather | solution.py:35
  227.6 18.7 %fusion.1 = f32[512,256]{1,0:T(8,128)} fusion(f32[512,256]{1,0:T(8,128)} %bitcast.22, f32[512,256]{1,0:T(8,128)} %param.11, f32[512,8192]{1,0:T(8,128)} %all-gather.3.cloned.1.call-done, f32[8192,256]{1,0:T(8,128)} %all-gather.5.cloned.1.call-done, f32[512]{0:T(512)S(1)} %add.14, f32[256]{0:T(256)S(1)} %add.13), kind=kOutput, calls=%fused_computation.2 | convolution fusion | flops 12885426176 | bytes 26741760 | tf_op jit(solution)/shard_map/dot_general | solution.py:34
  (2 shorter events, 0.0 us)
Async XLA Ops:
  6.5 30.1 %copy-start = (f32[100]{0:T(128)S(1)}, f32[100]{0:T(128)}, u32[]{:S(2)}) copy-start(f32[100]{0:T(128)} %param.16) | copy-start | bytes 1204
  6.5 120.7 %all-gather.5.cloned.1.call-start = ((), (), s32[]{:S(2)}) async-start(), calls=%async_computation.2 | async-start | bytes 9437184 | tf_op jit(solution)/shard_map/all_gather | solution.py:27
  7.3 220.4 %all-gather.3.cloned.1.call-start = ((), (), s32[]{:S(2)}) async-start(), calls=%async_computation.1 | async-start | bytes 17301504 | tf_op jit(solution)/shard_map/all_gather | solution.py:35
Sparse Core Ops, SparseCore 0:
  10.0 117.1 all-gather.4
  129.1 98.4 all-gather.2
where the time goes:
time: 253 us
  waiting for transfers between devices  187 us (74%)
  blocking collectives  27.5 us (11%)
  matrix products  22.9 us (9%)
  between operations  13.4 us (5%)
    all_gather x1, waiting for transfers between devices, local(): lax.all_gather(panel, 'row', axis=1, tiled=True)  100 us
    all_gather x1, waiting for transfers between devices, local(): column_panel = lax.all_gather(integrals, 'col', axis=0, tiled=True)  86.3 us
    all_to_all x1, blocking collectives, local(): lax.all_to_all(amplitudes, 'row', split_axis=1, concat_axis=0, tiled=True)  27.5 us
    dot_general x1, matrix products, local(): jnp.dot(lax.all_gather(panel, 'row', axis=1, tiled=True), column_panel, p...  18.7 us
  transfers between devices with their start and end apart: 2, of which 2 were waited for; matrix products, arithmetic and copies ran while one was open for 2% of the time, Pallas kernels for 0%

commit v1 on v0

v1 whole, which is shorter than its diff:
```python
import functools

import jax
import jax.numpy as jnp
from jax import lax
from jax.experimental import pallas as pl
from jax.experimental.pallas import tpu as pltpu
from jax.sharding import PartitionSpec as P

MESH = pl.DeviceIdType.MESH
F32, BF16 = jnp.float32, jnp.bfloat16
BASE = (0, 128, 384, 640, 896)
SIZE = (128, 256, 256, 256, 128)


def lookup(index_ref, table_ref):
    n = table_ref.shape[1]
    onehot = (lax.broadcasted_iota(jnp.int32, (n, index_ref.shape[1]), 0) == index_ref[...]).astype(F32)
    table = jnp.broadcast_to(table_ref[...], (8, n))
    return jnp.dot(table, onehot, precision=lax.Precision.HIGHEST, preferred_element_type=F32)


def kernel(
    a_ref, b_ref, other_ref, of_ref, os_ref, vf_ref, vs_ref, oe_ref, ve_ref,
    out_ref,
    abuf, ahi, alo, bbuf, bhi, blo, cbuf, rbuf, occ_row, occ_col, vsum,
    loc_sem, zs, zr, xs, xr, ss, sr, ys, yr, es, er, cs, cr, ts, tr,
):
    row, col = lax.axis_index("row"), lax.axis_index("col")
    xl, z, c = row // 16, (row // 2) % 8, row % 2
    xh, y = col // 4, col % 4

    def dev(xh, xl, y, z, c):
        return (xl * 16 + z * 2 + c, xh * 4 + y)

    px = ((xh, xl), (xh, 1 - xl), (1 - xh, 1 - xl), (1 - xh, xl))
    xdev = [dev(h, l, y, z, c) for h, l in px]
    zp, zm = (z + 1) % 8, (z + 7) % 8
    yp, ym = (y + 1) % 4, (y + 3) % 4
    zdev = (dev(xh, xl, y, zp, c), dev(xh, xl, y, zm, c))
    ydev = (dev(xh, xl, yp, z, c), dev(xh, xl, ym, z, c))
    sib = dev(xh, xl, y, z, 1 - c)

    def zof(s, p):
        return (z + 8 - s) % 8 if p == 0 else (z + s) % 8

    xi = [h * 2 + l for h, l in px]

    def remote(src, dst, send, recv, to):
        return pltpu.make_async_remote_copy(
            src_ref=src, dst_ref=dst, send_sem=send, recv_sem=recv, device_id=to, device_id_type=MESH
        )

    own_a = pltpu.make_async_copy(a_ref.at[:, xh, :, xl], abuf.at[z, xi[0], c], loc_sem.at[0])
    own_b = pltpu.make_async_copy(b_ref.at[:, xl], bbuf.at[0, y], loc_sem.at[1])
    own_o = pltpu.make_async_copy(other_ref, out_ref, loc_sem.at[2])
    own_a.start()
    own_b.start()
    own_o.start()

    barrier = pltpu.get_barrier_semaphore()
    for to in (*xdev[1:], *zdev, *ydev, sib):
        pl.semaphore_signal(barrier, inc=1, device_id=to, device_id_type=MESH)
    occ_row[0] = lookup(of_ref, oe_ref) + lookup(os_ref, oe_ref)
    vsum[0] = lookup(vf_ref, ve_ref) + lookup(vs_ref, ve_ref)
    pl.semaphore_wait(barrier, 8)

    sent = []

    def go(copy):
        copy.start()
        sent.append(copy)

    def z_send(s, q, d):
        where = (zof(s, d), xi[q], c)
        src = a_ref.at[:, xh, :, xl] if s == 0 and q == 0 else abuf.at[where]
        go(remote(src, abuf.at[where], zs.at[d, s, q], zr.at[d, s, q], zdev[d]))

    def z_wait(s, q, d):
        where = (zof(s, d), xi[q], c)
        remote(abuf.at[where], abuf.at[where], zs.at[d, s - 1, q], zr.at[d, s - 1, q], zdev[d]).wait_recv()

    def sib_copy(s, p, core):
        where = abuf.at[zof(s, p), :, core]
        i = 0 if s == 0 else 2 * s - 1 + p
        return remote(where, where, ss.at[i], sr.at[i], sib)

    for d in range(2):
        z_send(0, 0, d)
    for q in (1, 2, 3):
        go(
            remote(
                a_ref.at[:, px[q][0], :, px[q][1]], abuf.at[z, xi[0], c], xs.at[q - 1], xr.at[q - 1], xdev[q]
            )
        )
    for d in range(2):
        go(remote(b_ref.at[:, xl], bbuf.at[0, y], ys.at[0, d], yr.at[0, d], ydev[d]))
    go(remote(occ_row.at[0], occ_row.at[1], ts.at[0], tr.at[0], xdev[3]))
    go(remote(vsum.at[0], vsum.at[1], ts.at[1], tr.at[1], xdev[1]))
    own_a.wait()

    for q in (1, 2, 3):
        remote(abuf.at[z, xi[q], c], abuf.at[z, xi[q], c], xs.at[q - 1], xr.at[q - 1], xdev[q]).wait_recv()
        for d in range(2):
            z_send(0, q, d)
    go(sib_copy(0, 0, c))
    go(remote(b_ref.at[:, 1 - xl], bbuf.at[1, y], es.at[0], er.at[0], xdev[1]))

    def split_b(h, yy, g0, n):
        @pl.loop(0, n * 4)
        def _(i):
            g, r = g0 + i // 4, (i % 4) * 32
            r = pl.multiple_of(r, 32)
            v = bbuf[h, yy, g, pl.ds(r, 32), :]
            hi = v.astype(BF16)
            to = pl.ds(pl.multiple_of(yy * 512 + g * 128 + r, 32), 32)
            bhi[h, to, :] = hi
            blo[h, to, :] = (v - hi.astype(F32)).astype(BF16)

    def split_a(s):
        n = 1 if s in (0, 4) else 2

        @pl.loop(0, 16)
        def _(j):
            lanes = pl.ds(pl.multiple_of(j * 128, 128), 128)
            for p in range(n):
                for h in range(2):
                    v = abuf[zof(s, p), 2 * h : 2 * h + 2, :, :, j].reshape(64, 128)
                    hi = v.astype(BF16)
                    r = BASE[s] + h * (SIZE[s] // 2) + p * 64
                    ahi[r : r + 64, lanes] = hi
                    alo[r : r + 64, lanes] = (v - hi.astype(F32)).astype(BF16)

    mine = z * 2 + c
    half = pl.ds(pl.multiple_of(xl * 128, 128), 128)
    panel_h = jnp.where(xh == xl, 0, 1)

    def unit(s, h):
        r0, n = BASE[s], SIZE[s]
        rows = slice(r0, r0 + n)
        cbuf[h, rows, :] = (
            jnp.dot(alo[rows, :], bhi[h], preferred_element_type=F32)
            + jnp.dot(ahi[rows, :], blo[h], preferred_element_type=F32)
            + jnp.dot(ahi[rows, :], bhi[h], preferred_element_type=F32)
        )

        @pl.when(panel_h == h)
        def _():
            for p in range(n // 128):
                zz = zof(s, p)
                for k in range(2):
                    v = abuf[zz, 2 * k : 2 * k + 2, :, :, mine].reshape(64, 128)
                    for l in range(2):
                        o = occ_col[jnp.where(xh == k, 0, 1), pl.ds(pl.multiple_of(l * 256 + zz * 32, 32), 32), :]
                        d = vsum[h, 0:1, half] - o
                        r = r0 + k * (n // 2) + p * 64 + l * 32
                        cbuf[h, r : r + 32, half] += v[l * 32 : l * 32 + 32] * d

        def part(k):
            return cbuf.at[h, pl.ds(pl.multiple_of(r0 + k * (n // 2), 64), n // 2)]

        def to(q):
            return rbuf.at[q - 1, pl.ds(r0 // 2, n // 2)]

        if h == 0:
            go(remote(part(1 - xh), to(3), cs.at[s, 2], cr.at[s, 2], xdev[3]))
        else:
            go(remote(part(xh), to(1), cs.at[s, 0], cr.at[s, 0], xdev[1]))
            go(remote(part(1 - xh), to(2), cs.at[s, 1], cr.at[s, 1], xdev[2]))

    def finish(s):
        r0, n = BASE[s], SIZE[s]
        for q in (1, 2, 3):
            at = rbuf.at[q - 1, pl.ds(r0 // 2, n // 2)]
            remote(at, at, cs.at[s, q - 1], cr.at[s, q - 1], xdev[q]).wait_recv()
        for p in range(n // 128):
            zz = zof(s, p)
            for l in range(2):
                r = p * 64 + l * 32
                here = pl.ds(pl.multiple_of(r0 + xh * (n // 2) + r, 32), 32)
                there = pl.ds(r0 // 2 + r, 32)
                at = pl.ds(pl.multiple_of(l * 256 + zz * 32, 32), 32)
                total = cbuf[0, here, :] + rbuf[0, there, :] + rbuf[1, there, :] + rbuf[2, there, :]
                o = occ_col[0, at, :]
                d = vsum[0, 0:1, :] - jnp.concatenate([o, o], axis=1)
                out_ref[at, :] = (out_ref[at, :] + total) / d

    def y_wait(h, i):
        if i < 2:
            at = bbuf.at[h, (ym, yp)[i]]
        else:
            at = bbuf.at[h, (y + 2) % 4, pl.ds(2 * (i - 2), 2)]
        remote(at, at, ys.at[h, i], yr.at[h, i], ydev[i % 2]).wait_recv()

    def y_forward(h):
        for d in range(2):
            at = bbuf.at[h, (ym, yp)[d], pl.ds(2 * d, 2)]
            go(remote(at, at, ys.at[h, 2 + d], yr.at[h, 2 + d], ydev[d]))

    def z_step(s, qs):
        for q in qs:
            for d in range(2):
                if s == 4 and d != q // 2:
                    continue
                z_wait(s, q, d)
                if s < 3 or (s == 3 and d == q // 2):
                    z_send(s, q, d)

    def sib_send(s):
        for p in range(1 if s in (0, 4) else 2):
            go(sib_copy(s, p, c))

    def sib_wait(s):
        for p in range(1 if s in (0, 4) else 2):
            sib_copy(s, p, 1 - c).wait_recv()

    for k, at in ((0, occ_row.at[0]), (1, occ_row.at[1])):
        if k == 1:
            remote(at, at, ts.at[0], tr.at[0], xdev[3]).wait_recv()
        occ_col[k] = jnp.broadcast_to(at[0:1, :], (128, 512)).T
    remote(vsum.at[1], vsum.at[1], ts.at[1], tr.at[1], xdev[1]).wait_recv()
    own_b.wait()
    split_b(0, y, 0, 4)
    z_step(1, (0, 1))
    sib_wait(0)
    split_a(0)
    z_step(1, (2, 3))
    sib_send(1)
    y_wait(0, 0)
    y_wait(0, 1)
    y_forward(0)
    split_b(0, ym, 0, 4)
    split_b(0, yp, 0, 4)
    remote(bbuf.at[1, y], bbuf.at[1, y], es.at[0], er.at[0], xdev[1]).wait_recv()
    for d in range(2):
        go(remote(bbuf.at[1, y], bbuf.at[1, y], ys.at[1, d], yr.at[1, d], ydev[d]))
    sib_wait(1)
    split_a(1)
    split_b(1, y, 0, 4)
    z_step(2, (0, 1))
    y_wait(0, 2)
    y_wait(0, 3)
    split_b(0, (y + 2) % 4, 0, 4)
    unit(0, 0)
    unit(1, 0)
    z_step(2, (2, 3))
    sib_send(2)
    z_step(3, (0,))
    sib_wait(2)
    split_a(2)
    unit(2, 0)
    y_wait(1, 0)
    y_wait(1, 1)
    y_forward(1)
    z_step(3, (1,))
    split_b(1, ym, 0, 4)
    split_b(1, yp, 0, 4)
    z_step(3, (2, 3))
    sib_send(3)
    y_wait(1, 2)
    y_wait(1, 3)
    split_b(1, (y + 2) % 4, 0, 4)
    unit(0, 1)
    unit(1, 1)
    unit(2, 1)
    sib_wait(3)
    split_a(3)
    unit(3, 1)
    unit(3, 0)
    z_step(4, (0, 2, 1, 3))
    sib_send(4)
    own_o.wait()
    finish(0)
    sib_wait(4)
    split_a(4)
    unit(4, 1)
    unit(4, 0)
    for s in (1, 2, 3, 4):
        finish(s)
    for copy in sent:
        copy.wait_send()


def local(amplitudes, integrals, other_terms, of, os_, vf, vs, oe, ve):
    a = amplitudes.reshape(2, 8, 64, 128).transpose(0, 2, 1, 3).reshape(2, 2, 16, 2, 8, 128)
    b = integrals.reshape(4, 2, 128, 256)
    any_, vmem = pl.BlockSpec(memory_space=pl.ANY), pl.BlockSpec(memory_space=pltpu.VMEM)
    dma = pltpu.SemaphoreType.DMA
    return pl.pallas_call(
        kernel,
        out_shape=jax.ShapeDtypeStruct((512, 256), F32),
        in_specs=[any_, any_, any_] + [vmem] * 6,
        out_specs=vmem,
        scratch_shapes=[
            pltpu.VMEM((8, 4, 2, 2, 16, 8, 128), F32),
            pltpu.VMEM((1024, 2048), BF16),
            pltpu.VMEM((1024, 2048), BF16),
            pltpu.VMEM((2, 4, 4, 128, 256), F32),
            pltpu.VMEM((2, 2048, 256), BF16),
            pltpu.VMEM((2, 2048, 256), BF16),
            pltpu.VMEM((2, 1024, 256), F32),
            pltpu.VMEM((3, 512, 256), F32),
            pltpu.VMEM((2, 8, 512), F32),
            pltpu.VMEM((2, 512, 128), F32),
            pltpu.VMEM((2, 8, 256), F32),
            dma((3,)),
            dma((2, 4, 4)), dma((2, 4, 4)),
            dma((3,)), dma((3,)),
            dma((8,)), dma((8,)),
            dma((2, 4)), dma((2, 4)),
            dma((1,)), dma((1,)),
            dma((5, 3)), dma((5, 3)),
            dma((2,)), dma((2,)),
        ],
        compiler_params=pltpu.CompilerParams(
            collective_id=0, has_side_effects=True, vmem_limit_bytes=48 << 20
        ),
        cost_estimate=pl.CostEstimate(flops=6442450944, bytes_accessed=4 << 20, transcendentals=0),
    )(
        a, b, other_terms,
        of.reshape(1, -1), os_.reshape(1, -1), vf.reshape(1, -1), vs.reshape(1, -1),
        oe.reshape(1, -1), ve.reshape(1, -1),
    )


def solution(mesh):
    in_specs = (
        P(("col", "row"), None),
        P("col", "row"),
        P("col", "row"),
        P("col"),
        P("col"),
        P("row"),
        P("row"),
        P(),
        P(),
    )
    return jax.shard_map(local, mesh=mesh, in_specs=in_specs, out_specs=P("col", "row"), check_vma=False)
```

time: 253 us -> 77.4 us (0.31)
  waiting for transfers between devices: 187 us -> 0 us
  Pallas kernels: 0 us -> 71.6 us
  blocking collectives: 27.5 us -> 0 us
  matrix products: 22.9 us -> 0 us
  between operations: 13.4 us -> 0.04 us
  local copies, waits for them, and re-layouts: 1.79 us -> 5.5 us
    all_gather x2 -> x0, waiting for transfers between devices: 187 us -> none  [the longest x1 100 us: local(): lax.all_gather(panel, 'row', axis=1, tiled=True)]
    pallas_call x0 -> x1, Pallas kernels: none -> 71.6 us  [local(): pl.pallas_call(kernel, out_shape=jax.ShapeDtypeStruct((512, 256), F32), i...]
    all_to_all x1 -> x0, blocking collectives: 27.5 us -> none  [local(): lax.all_to_all(amplitudes, 'row', split_axis=1, concat_axis=0, tiled=True)]
    dot_general x5 -> x0, matrix products: 22.9 us -> none  [the longest x1 18.7 us: local(): jnp.dot(lax.all_gather(panel, 'row', axis=1, tiled=True), column_panel, p...]
    unnamed x3 -> x19, local copies, waits for them, and re-layouts: 0.7 us -> 5.49 us
  transfers between devices with their start and end apart: 2 -> 0, of which waited for: 2 -> 0; matrix products, arithmetic and copies ran while one was open for 2% -> 0% of each run, Pallas kernels for 0% -> 0%
where the time goes in v1:
time: 77.4 us; the launch traced here: 77.2 us
  Pallas kernels  71.6 us (93%)
  local copies, waits for them, and re-layouts  5.5 us (7%)
    pallas_call x1, Pallas kernels, local(): pl.pallas_call(kernel, out_shape=jax.ShapeDtypeStruct((512, 256), F32), i...  71.6 us
    unnamed x19, local copies, waits for them, and re-layouts  5.49 us

profile of v1, /device:TPU:1, one launch (start us, length us, event | category | flops | bytes accessed | tf_op | source)
XLA Modules:
  0.0 77.2 jit_solution(15818846842077814555)
XLA Ops:
  0.0 0.0 copy-start.8
  0.0 0.7 copy-done.8
  0.7 0.0 copy-start.3
  0.7 0.0 copy-start.4
  0.7 0.0 copy-start.5
  0.7 0.0 copy-start.6
  0.7 0.0 copy-start.7
  0.7 0.6 copy-done.3
  1.4 0.0 copy-done.4
  1.4 0.0 copy-done.5
  1.4 0.0 copy-done.6
  1.4 0.0 copy-done.7
  1.4 0.0 copy-start
  1.4 1.2 %copy-done = f32[1024,256]{1,0:T(8,128)S(1)} copy-done((f32[1024,256]{1,0:T(8,128)S(1)}, f32[1024,256]{1,0:T(8,128)}, u32[]{:S(2)}) %copy-start) | copy-done | bytes 1048600
  2.6 0.0 copy-start.1
  2.6 1.0 %copy-done.1 = f32[16,8192]{1,0:T(8,128)S(1)} copy-done((f32[16,8192]{1,0:T(8,128)S(1)}, f32[16,8192]{1,0:T(8,128)}, u32[]{:S(2)}) %copy-start.1) | copy-done | bytes 524312
  3.7 0.0 copy-start.2
  3.7 1.0 %copy-done.2 = f32[512,256]{1,0:T(8,128)S(1)} copy-done((f32[512,256]{1,0:T(8,128)S(1)}, f32[512,256]{1,0:T(8,128)}, u32[]{:S(2)}) %copy-start.2) | copy-done | bytes 524312
  4.7 71.6 %shard_map.91 = f32[512,256]{1,0:T(8,128)S(1)} custom-call(f32[2,2,16,2,8,128]{5,4,3,2,1,0:T(8,128)S(1)} %bitcast.12, f32[4,2,128,256]{3,2,1,0:T(8,128)S(1)} %bitcast.11, f32[512,256]{1,0:T(8,128)S(1)} %copy-done.2, s32[1,512]{1,0:T(1,128)S(1)} %bitcast.13, s32[1,512]{1,0:T(1,128)S(1)} %bitcast.14, s32[1,256]{1,0:T(1,128)S(1)} %bitcast.15, ...), custom_call_target="tpu_custom_call" | custom-call | flops 6442450944 | bytes 4194304 | tf_op jit(solution)/shard_map/pallas_call | solution.py:289
  76.4 0.8 %copy.11 = f32[512,256]{1,0:T(8,128)} copy(f32[512,256]{1,0:T(8,128)S(1)} %shard_map.91) | data formatting | bytes 1048576
  (1 shorter events, 0.0 us)
Async XLA Ops:
  0.0 0.7 copy-start.8
  0.7 0.7 copy-start.3
  0.7 0.7 copy-start.4
  0.7 0.7 copy-start.5
  0.7 0.7 copy-start.6
  0.7 0.7 copy-start.7
  1.4 1.2 %copy-start = (f32[1024,256]{1,0:T(8,128)S(1)}, f32[1024,256]{1,0:T(8,128)}, u32[]{:S(2)}) copy-start(f32[1024,256]{1,0:T(8,128)} %param.10) | copy-start | bytes 3145732
  2.6 1.0 %copy-start.1 = (f32[16,8192]{1,0:T(8,128)S(1)}, f32[16,8192]{1,0:T(8,128)}, u32[]{:S(2)}) copy-start(f32[16,8192]{1,0:T(8,128)} %param.9) | copy-start | bytes 1572868
  3.7 1.0 %copy-start.2 = (f32[512,256]{1,0:T(8,128)S(1)}, f32[512,256]{1,0:T(8,128)}, u32[]{:S(2)}) copy-start(f32[512,256]{1,0:T(8,128)} %other_ref.1) | copy-start | bytes 1572868

commit v2 on v0

v2 whole, which is shorter than its diff:
```python
import jax
import jax.numpy as jnp
from jax import lax
from jax.experimental import pallas as pl
from jax.experimental.pallas import tpu as pltpu
from jax.sharding import PartitionSpec as P

MESH = pl.DeviceIdType.MESH
F32, BF16 = jnp.float32, jnp.bfloat16
START = (0, 64, 192, 320, 448, 512)
ORDER = (
    (0, 0), (1, 0), (2, 0), (5, 0), (3, 0), (4, 0),
    (1, 1), (2, 1), (3, 1), (4, 1), (0, 1), (5, 1), (6, 1), (6, 0), (7, 1), (7, 0),
)


def lookup(index_ref, table_ref):
    n = table_ref.shape[-1]
    onehot = (lax.broadcasted_iota(jnp.int32, (n, index_ref.shape[1]), 0) == index_ref[...]).astype(F32)
    table = jnp.broadcast_to(table_ref[...].reshape(1, n), (8, n))
    return jnp.dot(table, onehot, precision=lax.Precision.HIGHEST, preferred_element_type=F32)


def kernel(
    a_ref, b_ref, other_ref, *refs
):
    small, out_ref, refs = refs[:6], refs[6], refs[7:]
    abuf, ahi, alo, bbuf, bhi, blo, cbuf, rbuf, occ_row, occ_col, vsum, obuf = refs[:12]
    small_v, (loc, zr, xr, sr, yr, er, cr, tr, os, sends) = refs[12:18], refs[18:]
    of_ref, os_ref, vf_ref, vs_ref, oe_ref, ve_ref = small_v
    row, col = lax.axis_index("row"), lax.axis_index("col")
    xl, z, c = row // 16, (row // 2) % 8, row % 2
    xh, y = col // 4, col % 4

    def dev(xh, xl, y, z, c):
        return (xl * 16 + z * 2 + c, xh * 4 + y)

    px = ((xh, xl), (xh, 1 - xl), (1 - xh, 1 - xl), (1 - xh, xl))
    xi = [h * 2 + l for h, l in px]
    xdev = [dev(h, l, y, z, c) for h, l in px]
    zp, zm = (z + 1) % 8, (z + 7) % 8
    yp, ym, y2 = (y + 1) % 4, (y + 3) % 4, (y + 2) % 4
    zdev = (dev(xh, xl, y, zp, c), dev(xh, xl, y, zm, c))
    ydev = (dev(xh, xl, yp, z, c), dev(xh, xl, ym, z, c))
    sib = dev(xh, xl, y, z, 1 - c)

    def sides(s):
        return range(1 if s in (0, 4) else 2)

    zs_of = [((z + 8 - s) % 8, (z + s) % 8) for s in range(5)]

    def zof(s, p):
        return zs_of[s][p]

    def remote(src, dst, recv, to):
        return pltpu.make_async_remote_copy(
            src_ref=src, dst_ref=dst, send_sem=sends, recv_sem=recv, device_id=to, device_id_type=MESH
        )

    sent = []

    def go(make):
        make().start()
        sent.append(make)

    barrier = pltpu.get_barrier_semaphore()
    for to in (*xdev[1:], *zdev, *ydev, sib):
        pl.semaphore_signal(barrier, inc=1, device_id=to, device_id_type=MESH)
    local = [pltpu.make_async_copy(src, dst, loc.at[i]) for i, (src, dst) in enumerate(zip(small, small_v))]
    own_a = pltpu.make_async_copy(a_ref.at[:, xh, :, xl], abuf.at[z, xi[0], c], loc.at[6])
    own_b = pltpu.make_async_copy(b_ref.at[:, xl], bbuf.at[0, y], loc.at[7])
    own_o = pltpu.make_async_copy(other_ref, obuf, loc.at[8])
    for copy in (own_a, *local, own_b, own_o):
        copy.start()

    def arrive(at, recv):
        remote(at, at, recv, sib).wait_recv()

    def z_sem(s, q, d):
        return zr.at[(s - 1) * 8 + d * 4 + q if s < 4 else 24 + q]

    def z_send(s, q, d):
        def make():
            where = abuf.at[zof(s, d), xi[q], c]
            src = a_ref.at[:, xh, :, xl] if s == 0 and q == 0 else where
            return remote(src, where, z_sem(s + 1, q, d), zdev[d])

        go(make)

    def z_step(s, q):
        for d in range(2):
            if s == 4 and d != q // 2:
                continue
            arrive(abuf.at[zof(s, d), xi[q], c], z_sem(s, q, d))
            if s < 3 or (s == 3 and d == q // 2):
                z_send(s, q, d)

    def x_send(q):
        go(lambda: remote(a_ref.at[:, px[q][0], :, px[q][1]], abuf.at[z, xi[0], c], xr.at[q - 1], xdev[q]))

    def x_step(q):
        arrive(abuf.at[z, xi[q], c], xr.at[q - 1])
        for d in range(2):
            z_send(0, q, d)

    def sib_at(s, p, k, core):
        if s == 4:
            return abuf.at[zof(s, 0), xi[k], core], sr.at[14 + k]
        where = abuf.at[zof(s, p), pl.ds(2 * (xh if k == 0 else 1 - xh), 2), core]
        return where, sr.at[2 * (0 if s == 0 else 2 * s - 1 + p) + k]

    def sib_send(s, k):
        for p in sides(s):

            def make(p=p):
                where, sem = sib_at(s, p, k, c)
                return remote(where, where, sem, sib)

            go(make)

    def sib_wait(s, k):
        for p in sides(s):
            arrive(*sib_at(s, p, k, 1 - c))

    def part(i, d):
        return pl.ds(2 * (i if d == 0 else 1 - i), 2)

    def y_send(h):
        for i in range(2):
            for d in range(2):

                def make(i=i, d=d):
                    src = b_ref.at[part(i, d), xl] if h == 0 else bbuf.at[h, y, part(i, d)]
                    return remote(src, bbuf.at[h, y, part(i, d)], yr.at[h * 6 + i * 2 + d], ydev[d])

                go(make)

    def y_wait(h, i):
        for d in range(2):
            arrive(bbuf.at[h, (ym, yp)[d], part(i, d)], yr.at[h * 6 + i * 2 + d])

    def y_forward(h):
        for d in range(2):

            def make(d=d):
                at = bbuf.at[h, (ym, yp)[d], part(0, d)]
                return remote(at, at, yr.at[h * 6 + 4 + d], ydev[d])

            go(make)

    def y_far(h):
        for d in range(2):
            arrive(bbuf.at[h, y2, part(0, d)], yr.at[h * 6 + 4 + d])

    def e_send():
        go(lambda: remote(b_ref.at[:, 1 - xl], bbuf.at[1, y], er, xdev[1]))

    def e_wait():
        arrive(bbuf.at[1, y], er)

    def split_b(h, yy):
        @pl.loop(0, 16)
        def _(i):
            g, r = i // 4, pl.multiple_of((i % 4) * 32, 32)
            v = bbuf[h, yy, g, pl.ds(r, 32), :]
            hi = v.astype(BF16)
            to = pl.ds(pl.multiple_of(yy * 512 + g * 128 + r, 32), 32)
            bhi[h, to, :] = hi
            blo[h, to, :] = (v - hi.astype(F32)).astype(BF16)

    def rows_at(s, p, k):
        return (64 * k if s in (0, 4) else 128 * k - 128) + 256 * s - (128 if s == 4 else 0) + 64 * p

    def split_a(s, k):
        @pl.loop(0, 16)
        def _(j):
            lanes = pl.ds(pl.multiple_of(j * 128, 128), 128)
            for p in sides(s):
                v = abuf[zof(s, p), pl.ds(2 * (xh if k == 0 else 1 - xh), 2), :, :, j].reshape(64, 128)
                hi = v.astype(BF16)
                r = rows_at(s, p, k)
                ahi[r : r + 64, lanes] = hi
                alo[r : r + 64, lanes] = (v - hi.astype(F32)).astype(BF16)

    mine = z * 2 + c
    panel_h = jnp.where(xh == xl, 0, 1)

    def block(b, h):
        r0 = pl.multiple_of(b * 128, 128)
        rows = pl.ds(r0, 128)
        cbuf[h, rows, :] = (
            jnp.dot(alo[rows, :], bhi[h], preferred_element_type=F32)
            + jnp.dot(ahi[rows, :], blo[h], preferred_element_type=F32)
            + jnp.dot(ahi[rows, :], bhi[h], preferred_element_type=F32)
        )

        @pl.when(panel_h == h)
        def _():
            lanes = pl.ds(pl.multiple_of(xl * 128, 128), 128)
            s, both = (b + 1) // 2, ((b == 0) | (b == 7)).astype(jnp.int32)
            for g in range(4):
                k = both * (g // 2) + (1 - both) * ((b + 1) % 2)
                up = (1 - both) * (g // 2)
                zz = (z + 8 + (2 * up - 1) * s) % 8
                x = 2 * (xh + k - 2 * xh * k) + g % 2
                v = abuf[zz, x, :, :, mine].reshape(32, 128)
                o = occ_col[k, pl.ds(pl.multiple_of(g % 2 * 256 + zz * 32, 32), 32), :]
                cbuf[h, pl.ds(r0 + 32 * g, 32), lanes] += v * (vsum[h, 0:1, lanes] - o)

    def c_copy(s, k, h):
        q = 3 if h == 0 else 1 + k
        size = START[s + 1] - START[s]
        src = cbuf.at[h, rows_at(s, 0, k) : rows_at(s, 0, k) + size]
        return remote(src, rbuf.at[q - 1, START[s] : START[s] + size], cr.at[s * 3 + q - 1], xdev[q])

    def c_send(s, k, h):
        go(lambda: c_copy(s, k, h))

    def finish(s):
        for k, h in ((1, 0), (0, 1), (1, 1)):
            c_copy(s, k, h).wait_recv()
        for p in sides(s):
            zz = zof(s, p)
            for l in range(2):
                r, t = rows_at(s, p, 0) + l * 32, START[s] + p * 64 + l * 32
                here, there = slice(r, r + 32), slice(t, t + 32)
                at = pl.ds(pl.multiple_of(l * 256 + zz * 32, 32), 32)
                total = (cbuf[0, here, :] + rbuf[2, there, :]) + (rbuf[0, there, :] + rbuf[1, there, :])
                o = occ_col[0, at, :]
                d = vsum[0, 0:1, :] - jnp.concatenate([o, o], axis=1)
                obuf[at, :] = (obuf[at, :] + total) / d
                pltpu.make_async_copy(obuf.at[at], out_ref.at[at], os).start()

    pl.semaphore_wait(barrier, 8)
    for d in range(2):
        z_send(0, 0, d)
    x_send(1)
    x_send(2)
    y_send(0)
    for copy in local:
        copy.wait()
    occ_row[0] = lookup(of_ref, oe_ref) + lookup(os_ref, oe_ref)
    vsum[0] = lookup(vf_ref, ve_ref) + lookup(vs_ref, ve_ref)
    go(lambda: remote(occ_row.at[0], occ_row.at[1], tr.at[0], xdev[3]))
    go(lambda: remote(vsum.at[0], vsum.at[1], tr.at[1], xdev[1]))
    x_step(1)
    x_step(2)
    x_send(3)
    e_send()
    z_step(1, 0)
    own_b.wait()
    split_b(0, y)
    y_wait(0, 0)
    y_forward(0)
    z_step(1, 1)
    x_step(3)
    own_a.wait()
    sib_send(0, 0)
    sib_send(0, 1)
    occ_col[0] = jnp.broadcast_to(occ_row[0, 0:1, :], (128, 512)).T
    arrive(occ_row.at[1], tr.at[0])
    arrive(vsum.at[1], tr.at[1])
    occ_col[1] = jnp.broadcast_to(occ_row[1, 0:1, :], (128, 512)).T
    z_step(1, 2)
    y_wait(0, 1)
    split_b(0, ym)
    split_b(0, yp)
    z_step(2, 0)
    for k in range(2):
        sib_wait(0, k)
        split_a(0, k)
    z_step(2, 1)
    e_wait()
    y_send(1)
    split_b(1, y)
    z_step(1, 3)
    sib_send(1, 0)
    sib_send(1, 1)
    y_far(0)
    split_b(0, y2)

    before = [[] for _ in ORDER]

    def at(j, f, *a):
        before[j].append(lambda: f(*a))

    at(1, c_send, 0, 1, 0)
    at(1, sib_wait, 1, 0)
    at(1, split_a, 1, 0)
    at(1, z_step, 2, 2)
    at(2, sib_wait, 1, 1)
    at(2, split_a, 1, 1)
    at(3, c_send, 1, 1, 0)
    at(3, y_wait, 1, 0)
    at(3, y_forward, 1)
    at(3, z_step, 3, 0)
    at(3, z_step, 3, 1)
    at(3, sib_send, 3, 0)
    at(3, sib_wait, 3, 0)
    at(3, split_a, 3, 0)
    at(4, z_step, 2, 3)
    at(4, sib_send, 2, 0)
    at(4, sib_send, 2, 1)
    at(4, y_wait, 1, 1)
    at(4, split_b, 1, ym)
    at(4, split_b, 1, yp)
    at(4, sib_wait, 2, 0)
    at(4, split_a, 2, 0)
    at(5, sib_wait, 2, 1)
    at(5, split_a, 2, 1)
    at(6, c_send, 2, 1, 0)
    at(6, z_step, 3, 2)
    at(6, y_far, 1)
    at(6, split_b, 1, y2)
    at(7, c_send, 1, 0, 1)
    at(8, c_send, 1, 1, 1)
    for q in (0, 2):
        at(8, z_step, 4, q)
        at(8, sib_send, 4, q)
    at(9, c_send, 2, 0, 1)
    at(10, c_send, 2, 1, 1)
    at(10, z_step, 3, 3)
    at(10, sib_send, 3, 1)
    at(11, c_send, 0, 0, 1)
    at(11, c_send, 0, 1, 1)
    at(12, c_send, 3, 0, 1)
    at(12, sib_wait, 3, 1)
    at(12, split_a, 3, 1)
    at(13, c_send, 3, 1, 1)
    at(14, c_send, 3, 1, 0)
    for q in (1, 3):
        at(14, z_step, 4, q)
        at(14, sib_send, 4, q)
    at(14, own_o.wait)
    for q in (0, 2, 1, 3):
        at(14, sib_wait, 4, q)
    at(14, split_a, 4, 0)
    at(14, split_a, 4, 1)
    at(15, c_send, 4, 0, 1)
    at(15, c_send, 4, 1, 1)

    @pl.loop(0, len(ORDER))
    def _(j):
        for k, steps in enumerate(before):
            if steps:

                @pl.when(j == k)
                def _():
                    for step in steps:
                        step()

        def pick(values):
            result = values[0]
            for i in range(1, len(values)):
                if values[i] != values[i - 1]:
                    result += (values[i] - values[i - 1]) * (j >= i).astype(jnp.int32)
            return result

        block(*(pick([o[i] for o in ORDER]) for i in range(2)))

    c_send(4, 1, 0)
    for s in range(5):
        finish(s)
    for make in sent:
        make().wait_send()
    pltpu.make_async_copy(obuf, out_ref, os).wait()


def local(amplitudes, integrals, other_terms, of, os_, vf, vs, oe, ve):
    a = amplitudes.reshape(2, 8, 64, 128).transpose(0, 2, 1, 3).reshape(2, 2, 16, 2, 8, 128)
    b = integrals.reshape(4, 2, 128, 256)
    small = [v.reshape(1, -1) for v in (of, os_, vf, vs, oe)] + [ve]
    hbm = pl.BlockSpec(memory_space=pltpu.HBM)
    dma = pltpu.SemaphoreType.DMA
    return pl.pallas_call(
        kernel,
        out_shape=jax.ShapeDtypeStruct((512, 256), F32),
        in_specs=[hbm] * 9,
        out_specs=pl.BlockSpec(memory_space=pl.ANY),
        scratch_shapes=[
            pltpu.VMEM((8, 4, 2, 2, 16, 8, 128), F32),
            pltpu.VMEM((1024, 2048), BF16),
            pltpu.VMEM((1024, 2048), BF16),
            pltpu.VMEM((2, 4, 4, 128, 256), F32),
            pltpu.VMEM((2, 2048, 256), BF16),
            pltpu.VMEM((2, 2048, 256), BF16),
            pltpu.VMEM((2, 1024, 256), F32),
            pltpu.VMEM((3, 512, 256), F32),
            pltpu.VMEM((2, 8, 512), F32),
            pltpu.VMEM((2, 512, 128), F32),
            pltpu.VMEM((2, 8, 256), F32),
            pltpu.VMEM((512, 256), F32),
            *[pltpu.VMEM(v.shape, v.dtype) for v in small],
            dma((9,)), dma((28,)), dma((3,)), dma((18,)), dma((12,)), dma, dma((15,)), dma((2,)), dma, dma,
        ],
        compiler_params=pltpu.CompilerParams(
            collective_id=0, has_side_effects=True, vmem_limit_bytes=62 << 20
        ),
        cost_estimate=pl.CostEstimate(flops=6442450944, bytes_accessed=4 << 20, transcendentals=0),
    )(a, b, other_terms, *small)


def solution(mesh):
    in_specs = (
        P(("col", "row"), None),
        P("col", "row"),
        P("col", "row"),
        P("col"),
        P("col"),
        P("row"),
        P("row"),
        P(),
        P(),
    )
    return jax.shard_map(local, mesh=mesh, in_specs=in_specs, out_specs=P("col", "row"), check_vma=False)
```

time: 253 us -> 71.1 us (0.28)
  waiting for transfers between devices: 187 us -> 0 us
  Pallas kernels: 0 us -> 69.1 us
  blocking collectives: 27.5 us -> 0 us
  matrix products: 22.9 us -> 0 us
  between operations: 13.4 us -> 0.01 us
    all_gather x2 -> x0, waiting for transfers between devices: 187 us -> none  [the longest x1 100 us: local(): lax.all_gather(panel, 'row', axis=1, tiled=True)]
    pallas_call x0 -> x1, Pallas kernels: none -> 69.1 us  [local(): pl.pallas_call(kernel, out_shape=jax.ShapeDtypeStruct((512, 256), F32), i...]
    all_to_all x1 -> x0, blocking collectives: 27.5 us -> none  [local(): lax.all_to_all(amplitudes, 'row', split_axis=1, concat_axis=0, tiled=True)]
    dot_general x5 -> x0, matrix products: 22.9 us -> none  [the longest x1 18.7 us: local(): jnp.dot(lax.all_gather(panel, 'row', axis=1, tiled=True), column_panel, p...]
  transfers between devices with their start and end apart: 2 -> 0, of which waited for: 2 -> 0; matrix products, arithmetic and copies ran while one was open for 2% -> 0% of each run, Pallas kernels for 0% -> 0%
where the time goes in v2:
time: 71.1 us; the launch traced here: 71 us
  Pallas kernels  69.1 us (97%)
  local copies, waits for them, and re-layouts  1.87 us (3%)
    pallas_call x1, Pallas kernels, local(): pl.pallas_call(kernel, out_shape=jax.ShapeDtypeStruct((512, 256), F32), i...  69.1 us
    unnamed x1, local copies, waits for them, and re-layouts  1.87 us

profile of v2, /device:TPU:1, one launch (start us, length us, event | category | flops | bytes accessed | tf_op | source)
XLA Modules:
  0.0 71.0 jit_solution(5393630912008354315)
XLA Ops:
  0.0 69.1 %shard_map.91 = f32[512,256]{1,0:T(8,128)} custom-call(f32[2,2,16,2,8,128]{5,4,3,2,1,0:T(8,128)} %bitcast.12, f32[4,2,128,256]{3,2,1,0:T(8,128)} %bitcast.11, f32[512,256]{1,0:T(8,128)} %other_ref.1, s32[1,512]{1,0:T(1,128)} %bitcast.13, s32[1,512]{1,0:T(1,128)} %bitcast.14, s32[1,256]{1,0:T(1,128)} %bitcast.15, s32[1,256]{1,0:T(1,128)} %bitcast.16, ...), custom_call_target="tpu_custom_call" | custom-call | flops 6442450944 | bytes 4194304 | tf_op jit(solution)/shard_map/pallas_call | solution.py:375
  69.1 1.9 %copy.11 = f32[512,256]{1,0:T(8,128)} copy(f32[512,256]{1,0:T(8,128)} %shard_map.91) | data formatting | bytes 1048576

commit v3 on v2

--- a/solution.py
+++ b/solution.py
@@ -8,9 +8,12 @@
 MESH = pl.DeviceIdType.MESH
 F32, BF16 = jnp.float32, jnp.bfloat16
 START = (0, 64, 192, 320, 448, 512)
+CHUNKS = ((0, 0, 256), (1, 0, 128), (1, 128, 128), (1, 0, 256))
+ALL0, LOW1, HIGH1, ALL1 = range(4)
 ORDER = (
-    (0, 0), (1, 0), (2, 0), (5, 0), (3, 0), (4, 0),
-    (1, 1), (2, 1), (3, 1), (4, 1), (0, 1), (5, 1), (6, 1), (6, 0), (7, 1), (7, 0),
+    (0, 1, ALL0), (2, 2, ALL0), (6, 2, ALL0), (2, 2, LOW1), (0, 1, LOW1), (6, 2, LOW1), (12, 1, ALL0), (12, 1, LOW1),
+    (2, 2, HIGH1), (6, 2, HIGH1), (0, 1, HIGH1), (12, 1, HIGH1), (15, 0, ALL1), (15, 0, ALL0), (10, 1, ALL1),
+    (14, 0, ALL1), (14, 0, ALL0), (10, 1, ALL0),
 )
 
 
@@ -87,12 +90,20 @@
 
         go(make)
 
+    def z_wait(s, q):
+        for d in range(2):
+            if s < 4 or d == q % 2:
+                arrive(abuf.at[zof(s, d), xi[q], c], z_sem(s, q, d))
+
+    def z_forward(s, q):
+        for d in range(2):
+            if s < 3 or d == q % 2:
+                z_send(s, q, d)
+
     def z_step(s, q):
-        for d in range(2):
-            if s == 4 and d != q // 2:
-                continue
+        for d in (q % 2, 1 - q % 2):
             arrive(abuf.at[zof(s, d), xi[q], c], z_sem(s, q, d))
-            if s < 3 or (s == 3 and d == q // 2):
+            if s < 3 or d == q % 2:
                 z_send(s, q, d)
 
     def x_send(q):
@@ -122,51 +133,59 @@
         for p in sides(s):
             arrive(*sib_at(s, p, k, 1 - c))
 
+    def b_at(n, yy, groups=slice(None)):
+        h, l0, nl = CHUNKS[n]
+        return bbuf.at[h, yy, groups, :, l0 : l0 + nl]
+
     def part(i, d):
         return pl.ds(2 * (i if d == 0 else 1 - i), 2)
 
-    def y_send(h):
-        for i in range(2):
-            for d in range(2):
-
-                def make(i=i, d=d):
-                    src = b_ref.at[part(i, d), xl] if h == 0 else bbuf.at[h, y, part(i, d)]
-                    return remote(src, bbuf.at[h, y, part(i, d)], yr.at[h * 6 + i * 2 + d], ydev[d])
-
-                go(make)
-
-    def y_wait(h, i):
-        for d in range(2):
-            arrive(bbuf.at[h, (ym, yp)[d], part(i, d)], yr.at[h * 6 + i * 2 + d])
-
-    def y_forward(h):
+    def y_send(n, i):
+        h, l0, nl = CHUNKS[n]
         for d in range(2):
 
             def make(d=d):
-                at = bbuf.at[h, (ym, yp)[d], part(0, d)]
-                return remote(at, at, yr.at[h * 6 + 4 + d], ydev[d])
+                src = b_ref.at[part(i, d), xl, :, l0 : l0 + nl] if h == 0 else b_at(n, y, part(i, d))
+                return remote(src, b_at(n, y, part(i, d)), yr.at[n * 6 + i * 2 + d], ydev[d])
 
             go(make)
 
-    def y_far(h):
-        for d in range(2):
-            arrive(bbuf.at[h, y2, part(0, d)], yr.at[h * 6 + 4 + d])
-
-    def e_send():
-        go(lambda: remote(b_ref.at[:, 1 - xl], bbuf.at[1, y], er, xdev[1]))
-
-    def e_wait():
-        arrive(bbuf.at[1, y], er)
-
-    def split_b(h, yy):
+    def y_wait(n, i):
+        for d in range(2):
+            arrive(b_at(n, (ym, yp)[d], part(i, d)), yr.at[n * 6 + i * 2 + d])
+
+    def y_forward(n):
+        for d in range(2):
+
+            def make(d=d):
+                at = b_at(n, (ym, yp)[d], part(0, d))
+                return remote(at, at, yr.at[n * 6 + 4 + d], ydev[d])
+
+            go(make)
+
+    def y_far(n):
+        for d in range(2):
+            arrive(b_at(n, y2, part(0, d)), yr.at[n * 6 + 4 + d])
+
+    def e_send(n):
+        h, l0, nl = CHUNKS[n]
+        go(lambda: remote(b_ref.at[:, 1 - xl, :, l0 : l0 + nl], b_at(n, y), er.at[n - LOW1], xdev[1]))
+
+    def e_wait(n):
+        arrive(b_at(n, y), er.at[n - LOW1])
+
+    def split_b(n, yy):
+        h, l0, nl = CHUNKS[n]
+        lanes = slice(l0, l0 + nl)
+
         @pl.loop(0, 16)
         def _(i):
             g, r = i // 4, pl.multiple_of((i % 4) * 32, 32)
-            v = bbuf[h, yy, g, pl.ds(r, 32), :]
+            v = bbuf[h, yy, g, pl.ds(r, 32), lanes]
             hi = v.astype(BF16)
             to = pl.ds(pl.multiple_of(yy * 512 + g * 128 + r, 32), 32)
-            bhi[h, to, :] = hi
-            blo[h, to, :] = (v - hi.astype(F32)).astype(BF16)
+            bhi[h, to, lanes] = hi
+            blo[h, to, lanes] = (v - hi.astype(F32)).astype(BF16)
 
     def rows_at(s, p, k):
         return (64 * k if s in (0, 4) else 128 * k - 128) + 256 * s - (128 if s == 4 else 0) + 64 * p
@@ -185,40 +204,64 @@
     mine = z * 2 + c
     panel_h = jnp.where(xh == xl, 0, 1)
 
-    def block(b, h):
-        r0 = pl.multiple_of(b * 128, 128)
-        rows = pl.ds(r0, 128)
-        cbuf[h, rows, :] = (
-            jnp.dot(alo[rows, :], bhi[h], preferred_element_type=F32)
-            + jnp.dot(ahi[rows, :], blo[h], preferred_element_type=F32)
-            + jnp.dot(ahi[rows, :], bhi[h], preferred_element_type=F32)
-        )
-
-        @pl.when(panel_h == h)
+    def block(first, scale, n):
+        h = (n != ALL0).astype(jnp.int32)
+        low, high = n != HIGH1, n != LOW1
+        r0 = pl.multiple_of(first * 64, 64)
+
+        def product(size):
+            rows = pl.ds(r0, size)
+            total = (
+                jnp.dot(alo[rows, :], bhi[h], preferred_element_type=F32)
+                + jnp.dot(ahi[rows, :], blo[h], preferred_element_type=F32)
+                + jnp.dot(ahi[rows, :], bhi[h], preferred_element_type=F32)
+            )
+
+            @pl.when(low)
+            def _():
+                cbuf[h, rows, :128] = total[:, :128]
+
+            @pl.when(high)
+            def _():
+                cbuf[h, rows, 128:] = total[:, 128:]
+
+        for k in range(3):
+            pl.when(scale == k)(lambda k=k: product(64 << k))
+
+        @pl.when((panel_h == h) & ((low & (xl == 0)) | (high & (xl == 1))))
         def _():
             lanes = pl.ds(pl.multiple_of(xl * 128, 128), 128)
-            s, both = (b + 1) // 2, ((b == 0) | (b == 7)).astype(jnp.int32)
-            for g in range(4):
-                k = both * (g // 2) + (1 - both) * ((b + 1) % 2)
+
+            @pl.loop(0, 2 + 2 * scale + 2 * (scale // 2))
+            def _(i):
+                bb, g = (2 * first + i) // 4, (2 * first + i) % 4
+                s, both = (bb + 1) // 2, ((bb == 0) | (bb == 7)).astype(jnp.int32)
+                k = both * (g // 2) + (1 - both) * ((bb + 1) % 2)
                 up = (1 - both) * (g // 2)
                 zz = (z + 8 + (2 * up - 1) * s) % 8
                 x = 2 * (xh + k - 2 * xh * k) + g % 2
                 v = abuf[zz, x, :, :, mine].reshape(32, 128)
                 o = occ_col[k, pl.ds(pl.multiple_of(g % 2 * 256 + zz * 32, 32), 32), :]
-                cbuf[h, pl.ds(r0 + 32 * g, 32), lanes] += v * (vsum[h, 0:1, lanes] - o)
-
-    def c_copy(s, k, h):
+                cbuf[h, pl.ds(pl.multiple_of(r0 + 32 * i, 32), 32), lanes] += v * (vsum[h, 0:1, lanes] - o)
+
+    def c_copy(s, k, n):
+        h, l0, nl = CHUNKS[n]
         q = 3 if h == 0 else 1 + k
-        size = START[s + 1] - START[s]
-        src = cbuf.at[h, rows_at(s, 0, k) : rows_at(s, 0, k) + size]
-        return remote(src, rbuf.at[q - 1, START[s] : START[s] + size], cr.at[s * 3 + q - 1], xdev[q])
-
-    def c_send(s, k, h):
-        go(lambda: c_copy(s, k, h))
+        size, lanes = START[s + 1] - START[s], slice(l0, l0 + nl)
+        src = cbuf.at[h, rows_at(s, 0, k) : rows_at(s, 0, k) + size, lanes]
+        dst = rbuf.at[q - 1, START[s] : START[s] + size, lanes]
+        return remote(src, dst, cr.at[s * 6 + 2 * (q - 1) + (1 if l0 else 0)], xdev[q])
+
+    c_sent = []
+
+    def c_send(*what):
+        go(lambda: c_copy(*what))
+        c_sent.append(what)
 
     def finish(s):
-        for k, h in ((1, 0), (0, 1), (1, 1)):
-            c_copy(s, k, h).wait_recv()
+        for what in c_sent:
+            if what[0] == s:
+                c_copy(*what).wait_recv()
         for p in sides(s):
             zz = zof(s, p)
             for l in range(2):
@@ -234,120 +277,147 @@
     pl.semaphore_wait(barrier, 8)
     for d in range(2):
         z_send(0, 0, d)
-    x_send(1)
-    x_send(2)
-    y_send(0)
+    for q in (1, 2, 3):
+        x_send(q)
+    y_send(ALL0, 0)
+    y_send(ALL0, 1)
     for copy in local:
         copy.wait()
     occ_row[0] = lookup(of_ref, oe_ref) + lookup(os_ref, oe_ref)
     vsum[0] = lookup(vf_ref, ve_ref) + lookup(vs_ref, ve_ref)
     go(lambda: remote(occ_row.at[0], occ_row.at[1], tr.at[0], xdev[3]))
     go(lambda: remote(vsum.at[0], vsum.at[1], tr.at[1], xdev[1]))
+    e_send(LOW1)
+    e_send(HIGH1)
+    z_step(1, 0)
+    x_step(2)
     x_step(1)
-    x_step(2)
-    x_send(3)
-    e_send()
-    z_step(1, 0)
+    y_wait(ALL0, 0)
+    y_forward(ALL0)
     own_b.wait()
-    split_b(0, y)
-    y_wait(0, 0)
-    y_forward(0)
-    z_step(1, 1)
+    split_b(ALL0, y)
     x_step(3)
     own_a.wait()
     sib_send(0, 0)
     sib_send(0, 1)
+    z_step(1, 2)
+    e_wait(LOW1)
+    y_send(LOW1, 0)
+    y_send(LOW1, 1)
     occ_col[0] = jnp.broadcast_to(occ_row[0, 0:1, :], (128, 512)).T
     arrive(occ_row.at[1], tr.at[0])
     arrive(vsum.at[1], tr.at[1])
     occ_col[1] = jnp.broadcast_to(occ_row[1, 0:1, :], (128, 512)).T
-    z_step(1, 2)
-    y_wait(0, 1)
-    split_b(0, ym)
-    split_b(0, yp)
-    z_step(2, 0)
+    y_wait(ALL0, 1)
+    split_b(ALL0, ym)
+    split_b(ALL0, yp)
+    z_step(1, 1)
     for k in range(2):
         sib_wait(0, k)
         split_a(0, k)
-    z_step(2, 1)
-    e_wait()
-    y_send(1)
-    split_b(1, y)
+    split_b(LOW1, y)
     z_step(1, 3)
+    sib_send(1, 1)
     sib_send(1, 0)
-    sib_send(1, 1)
-    y_far(0)
-    split_b(0, y2)
+    y_far(ALL0)
+    split_b(ALL0, y2)
+    z_step(2, 2)
 
     before = [[] for _ in ORDER]
 
     def at(j, f, *a):
         before[j].append(lambda: f(*a))
 
-    at(1, c_send, 0, 1, 0)
+    at(1, c_send, 0, 1, ALL0)
+    at(1, sib_wait, 1, 1)
+    at(1, split_a, 1, 1)
     at(1, sib_wait, 1, 0)
     at(1, split_a, 1, 0)
-    at(1, z_step, 2, 2)
-    at(2, sib_wait, 1, 1)
-    at(2, split_a, 1, 1)
-    at(3, c_send, 1, 1, 0)
-    at(3, y_wait, 1, 0)
-    at(3, y_forward, 1)
-    at(3, z_step, 3, 0)
-    at(3, z_step, 3, 1)
-    at(3, sib_send, 3, 0)
-    at(3, sib_wait, 3, 0)
-    at(3, split_a, 3, 0)
-    at(4, z_step, 2, 3)
-    at(4, sib_send, 2, 0)
-    at(4, sib_send, 2, 1)
-    at(4, y_wait, 1, 1)
-    at(4, split_b, 1, ym)
-    at(4, split_b, 1, yp)
-    at(4, sib_wait, 2, 0)
-    at(4, split_a, 2, 0)
-    at(5, sib_wait, 2, 1)
-    at(5, split_a, 2, 1)
-    at(6, c_send, 2, 1, 0)
-    at(6, z_step, 3, 2)
-    at(6, y_far, 1)
-    at(6, split_b, 1, y2)
-    at(7, c_send, 1, 0, 1)
-    at(8, c_send, 1, 1, 1)
-    for q in (0, 2):
-        at(8, z_step, 4, q)
-        at(8, sib_send, 4, q)
-    at(9, c_send, 2, 0, 1)
-    at(10, c_send, 2, 1, 1)
-    at(10, z_step, 3, 3)
-    at(10, sib_send, 3, 1)
-    at(11, c_send, 0, 0, 1)
-    at(11, c_send, 0, 1, 1)
-    at(12, c_send, 3, 0, 1)
-    at(12, sib_wait, 3, 1)
-    at(12, split_a, 3, 1)
-    at(13, c_send, 3, 1, 1)
-    at(14, c_send, 3, 1, 0)
-    for q in (1, 3):
-        at(14, z_step, 4, q)
-        at(14, sib_send, 4, q)
-    at(14, own_o.wait)
-    for q in (0, 2, 1, 3):
-        at(14, sib_wait, 4, q)
-    at(14, split_a, 4, 0)
-    at(14, split_a, 4, 1)
-    at(15, c_send, 4, 0, 1)
-    at(15, c_send, 4, 1, 1)
+    at(1, y_wait, LOW1, 0)
+    at(1, y_forward, LOW1)
+    at(1, e_wait, HIGH1)
+    at(1, y_send, HIGH1, 0)
+    at(1, y_send, HIGH1, 1)
+    at(1, split_b, HIGH1, y)
+    at(2, c_send, 1, 1, ALL0)
+    at(2, z_step, 2, 3)
+    at(2, sib_send, 2, 1)
+    at(2, z_wait, 2, 0)
+    at(2, z_step, 2, 1)
+    at(2, sib_send, 2, 0)
+    at(2, y_wait, LOW1, 1)
+    at(2, split_b, LOW1, ym)
+    at(2, split_b, LOW1, yp)
+    at(2, sib_wait, 2, 1)
+    at(2, split_a, 2, 1)
+    at(2, sib_wait, 2, 0)
+    at(2, split_a, 2, 0)
+    at(3, c_send, 2, 1, ALL0)
+    at(3, y_far, LOW1)
+    at(3, split_b, LOW1, y2)
+    at(4, c_send, 1, 0, LOW1)
+    at(4, c_send, 1, 1, LOW1)
+    at(4, z_step, 3, 2)
+    at(5, c_send, 0, 0, LOW1)
+    at(5, c_send, 0, 1, LOW1)
+    at(6, c_send, 2, 0, LOW1)
+    at(6, c_send, 2, 1, LOW1)
+    at(6, y_wait, HIGH1, 0)
+    at(6, y_forward, HIGH1)
+    at(6, z_step, 3, 3)
+    at(6, z_forward, 2, 0)
+    at(6, sib_send, 3, 1)
+    at(6, sib_wait, 3, 1)
+    at(6, split_a, 3, 1)
+    at(7, c_send, 3, 1, ALL0)
+    at(7, z_step, 3, 1)
+    at(8, c_send, 3, 1, LOW1)
+    at(8, y_wait, HIGH1, 1)
+    at(8, split_b, HIGH1, ym)
+    at(8, split_b, HIGH1, yp)
+    at(8, y_far, HIGH1)
+    at(8, split_b, HIGH1, y2)
+    at(9, c_send, 1, 0, HIGH1)
+    at(9, c_send, 1, 1, HIGH1)
+    for q in (2, 3):
+        at(9, z_wait, 4, q)
+        at(9, sib_send, 4, q)
+    at(10, c_send, 2, 0, HIGH1)
+    at(10, c_send, 2, 1, HIGH1)
+    at(11, c_send, 0, 0, HIGH1)
+    at(11, c_send, 0, 1, HIGH1)
+    at(11, z_step, 3, 0)
+    at(11, sib_send, 3, 0)
+    at(12, c_send, 3, 1, HIGH1)
+    for q in (2, 3):
+        at(12, sib_wait, 4, q)
+    at(12, split_a, 4, 1)
+    at(13, c_send, 4, 1, ALL1)
+    at(14, c_send, 4, 1, ALL0)
+    at(14, sib_wait, 3, 0)
+    at(14, split_a, 3, 0)
+    at(15, c_send, 3, 0, ALL1)
+    for q in (0, 1):
+        at(15, z_wait, 4, q)
+        at(15, sib_send, 4, q)
+    at(15, own_o.wait)
+    for q in (0, 1):
+        at(15, sib_wait, 4, q)
+    at(15, split_a, 4, 0)
+    at(16, c_send, 4, 0, ALL1)
 
     @pl.loop(0, len(ORDER))
     def _(j):
-        for k, steps in enumerate(before):
-            if steps:
-
-                @pl.when(j == k)
-                def _():
-                    for step in steps:
-                        step()
+        def run(first, end):
+            if end - first == 1:
+                for step in before[first]:
+                    step()
+            else:
+                middle = (first + end) // 2
+                pl.when(j < middle)(lambda: run(first, middle))
+                pl.when(j >= middle)(lambda: run(middle, end))
+
+        run(0, len(ORDER))
 
         def pick(values):
             result = values[0]
@@ -356,9 +426,8 @@
                     result += (values[i] - values[i - 1]) * (j >= i).astype(jnp.int32)
             return result
 
-        block(*(pick([o[i] for o in ORDER]) for i in range(2)))
-
-    c_send(4, 1, 0)
+        block(*(pick([o[i] for o in ORDER]) for i in range(3)))
+
     for s in range(5):
         finish(s)
     for make in sent:
@@ -391,7 +460,7 @@
             pltpu.VMEM((2, 8, 256), F32),
             pltpu.VMEM((512, 256), F32),
             *[pltpu.VMEM(v.shape, v.dtype) for v in small],
-            dma((9,)), dma((28,)), dma((3,)), dma((18,)), dma((12,)), dma, dma((15,)), dma((2,)), dma, dma,
+            dma((9,)), dma((28,)), dma((3,)), dma((18,)), dma((18,)), dma((2,)), dma((30,)), dma((2,)), dma, dma,
         ],
         compiler_params=pltpu.CompilerParams(
             collective_id=0, has_side_effects=True, vmem_limit_bytes=62 << 20

time: 71.1 us -> 66.6 us (0.937)
  Pallas kernels: 69.1 us -> 64.6 us
    pallas_call x1, Pallas kernels: 69.1 us -> 64.6 us  [local(): pl.pallas_call(kernel, out_shape=jax.ShapeDtypeStruct((512, 256), F32), i...]
where the time goes in v3:
time: 66.6 us; the launch traced here: 66.5 us
  Pallas kernels  64.6 us (97%)
  local copies, waits for them, and re-layouts  1.87 us (3%)
    pallas_call x1, Pallas kernels, local(): pl.pallas_call(kernel, out_shape=jax.ShapeDtypeStruct((512, 256), F32), i...  64.6 us
    unnamed x1, local copies, waits for them, and re-layouts  1.87 us

profile of v3, /device:TPU:1, one launch (start us, length us, event | category | flops | bytes accessed | tf_op | source)
XLA Modules:
  0.0 66.5 jit_solution(10894146053159859164)
XLA Ops:
  0.0 64.6 %shard_map.91 = f32[512,256]{1,0:T(8,128)} custom-call(f32[2,2,16,2,8,128]{5,4,3,2,1,0:T(8,128)} %bitcast.12, f32[4,2,128,256]{3,2,1,0:T(8,128)} %bitcast.11, f32[512,256]{1,0:T(8,128)} %other_ref.1, s32[1,512]{1,0:T(1,128)} %bitcast.13, s32[1,512]{1,0:T(1,128)} %bitcast.14, s32[1,256]{1,0:T(1,128)} %bitcast.15, s32[1,256]{1,0:T(1,128)} %bitcast.16, ...), custom_call_target="tpu_custom_call" | custom-call | flops 6442450944 | bytes 4194304 | tf_op jit(solution)/shard_map/pallas_call | solution.py:444
  64.6 1.9 %copy.11 = f32[512,256]{1,0:T(8,128)} copy(f32[512,256]{1,0:T(8,128)} %shard_map.91) | data formatting | bytes 1048576

commit v4 on v3

--- a/solution.py
+++ b/solution.py
@@ -11,9 +11,9 @@
 CHUNKS = ((0, 0, 256), (1, 0, 128), (1, 128, 128), (1, 0, 256))
 ALL0, LOW1, HIGH1, ALL1 = range(4)
 ORDER = (
-    (0, 1, ALL0), (2, 2, ALL0), (6, 2, ALL0), (2, 2, LOW1), (0, 1, LOW1), (6, 2, LOW1), (12, 1, ALL0), (12, 1, LOW1),
-    (2, 2, HIGH1), (6, 2, HIGH1), (0, 1, HIGH1), (12, 1, HIGH1), (15, 0, ALL1), (15, 0, ALL0), (10, 1, ALL1),
-    (14, 0, ALL1), (14, 0, ALL0), (10, 1, ALL0),
+    (0, 1, ALL0), (2, 2, ALL0), (2, 2, LOW1), (0, 1, LOW1), (6, 2, ALL0), (6, 2, LOW1), (12, 1, ALL0),
+    (2, 2, HIGH1), (6, 2, HIGH1), (0, 1, HIGH1), (12, 1, ALL1), (15, 0, ALL0), (10, 1, ALL1), (15, 0, ALL1),
+    (14, 0, ALL1), (10, 1, ALL0), (14, 0, ALL0),
 )
 
 
@@ -90,19 +90,12 @@
 
         go(make)
 
-    def z_wait(s, q):
-        for d in range(2):
-            if s < 4 or d == q % 2:
-                arrive(abuf.at[zof(s, d), xi[q], c], z_sem(s, q, d))
-
-    def z_forward(s, q):
-        for d in range(2):
-            if s < 3 or d == q % 2:
-                z_send(s, q, d)
+    def z_wait(s, q, d):
+        arrive(abuf.at[zof(s, d), xi[q], c], z_sem(s, q, d))
 
     def z_step(s, q):
         for d in (q % 2, 1 - q % 2):
-            arrive(abuf.at[zof(s, d), xi[q], c], z_sem(s, q, d))
+            z_wait(s, q, d)
             if s < 3 or d == q % 2:
                 z_send(s, q, d)
 
@@ -342,69 +335,74 @@
     at(2, c_send, 1, 1, ALL0)
     at(2, z_step, 2, 3)
     at(2, sib_send, 2, 1)
-    at(2, z_wait, 2, 0)
-    at(2, z_step, 2, 1)
+    for q in (0, 1):
+        for d in (0, 1):
+            at(2, z_wait, 2, q, d)
+        at(2, z_send, 2, q, q)
     at(2, sib_send, 2, 0)
     at(2, y_wait, LOW1, 1)
     at(2, split_b, LOW1, ym)
     at(2, split_b, LOW1, yp)
-    at(2, sib_wait, 2, 1)
-    at(2, split_a, 2, 1)
-    at(2, sib_wait, 2, 0)
-    at(2, split_a, 2, 0)
-    at(3, c_send, 2, 1, ALL0)
-    at(3, y_far, LOW1)
-    at(3, split_b, LOW1, y2)
-    at(4, c_send, 1, 0, LOW1)
-    at(4, c_send, 1, 1, LOW1)
+    at(2, y_far, LOW1)
+    at(2, split_b, LOW1, y2)
+    at(3, c_send, 1, 0, LOW1)
+    at(3, c_send, 1, 1, LOW1)
+    at(4, c_send, 0, 0, LOW1)
+    at(4, c_send, 0, 1, LOW1)
     at(4, z_step, 3, 2)
-    at(5, c_send, 0, 0, LOW1)
-    at(5, c_send, 0, 1, LOW1)
+    at(4, sib_wait, 2, 1)
+    at(4, split_a, 2, 1)
+    at(4, sib_wait, 2, 0)
+    at(4, split_a, 2, 0)
+    at(5, c_send, 2, 1, ALL0)
+    at(5, y_wait, HIGH1, 0)
+    at(5, y_forward, HIGH1)
     at(6, c_send, 2, 0, LOW1)
     at(6, c_send, 2, 1, LOW1)
-    at(6, y_wait, HIGH1, 0)
-    at(6, y_forward, HIGH1)
     at(6, z_step, 3, 3)
-    at(6, z_forward, 2, 0)
+    for q in (0, 1):
+        at(6, z_send, 2, q, 1 - q)
     at(6, sib_send, 3, 1)
     at(6, sib_wait, 3, 1)
     at(6, split_a, 3, 1)
     at(7, c_send, 3, 1, ALL0)
-    at(7, z_step, 3, 1)
-    at(8, c_send, 3, 1, LOW1)
-    at(8, y_wait, HIGH1, 1)
-    at(8, split_b, HIGH1, ym)
-    at(8, split_b, HIGH1, yp)
-    at(8, y_far, HIGH1)
-    at(8, split_b, HIGH1, y2)
-    at(9, c_send, 1, 0, HIGH1)
-    at(9, c_send, 1, 1, HIGH1)
+    for q in (0, 1):
+        at(7, z_wait, 3, q, q)
+        at(7, z_send, 3, q, q)
+    at(7, y_wait, HIGH1, 1)
+    at(7, split_b, HIGH1, ym)
+    at(7, split_b, HIGH1, yp)
+    at(7, y_far, HIGH1)
+    at(7, split_b, HIGH1, y2)
+    at(8, c_send, 1, 0, HIGH1)
+    at(8, c_send, 1, 1, HIGH1)
     for q in (2, 3):
-        at(9, z_wait, 4, q)
-        at(9, sib_send, 4, q)
-    at(10, c_send, 2, 0, HIGH1)
-    at(10, c_send, 2, 1, HIGH1)
-    at(11, c_send, 0, 0, HIGH1)
-    at(11, c_send, 0, 1, HIGH1)
-    at(11, z_step, 3, 0)
-    at(11, sib_send, 3, 0)
-    at(12, c_send, 3, 1, HIGH1)
+        at(8, z_wait, 4, q, q % 2)
+        at(8, sib_send, 4, q)
+    at(9, c_send, 2, 0, HIGH1)
+    at(9, c_send, 2, 1, HIGH1)
+    at(10, c_send, 0, 0, HIGH1)
+    at(10, c_send, 0, 1, HIGH1)
+    for q in (0, 1):
+        at(10, z_wait, 3, q, 1 - q)
+    at(10, sib_send, 3, 0)
+    at(11, c_send, 3, 1, ALL1)
     for q in (2, 3):
-        at(12, sib_wait, 4, q)
-    at(12, split_a, 4, 1)
-    at(13, c_send, 4, 1, ALL1)
-    at(14, c_send, 4, 1, ALL0)
-    at(14, sib_wait, 3, 0)
-    at(14, split_a, 3, 0)
-    at(15, c_send, 3, 0, ALL1)
-    for q in (0, 1):
-        at(15, z_wait, 4, q)
-        at(15, sib_send, 4, q)
-    at(15, own_o.wait)
-    for q in (0, 1):
-        at(15, sib_wait, 4, q)
-    at(15, split_a, 4, 0)
-    at(16, c_send, 4, 0, ALL1)
+        at(11, sib_wait, 4, q)
+    at(11, split_a, 4, 1)
+    at(12, c_send, 4, 1, ALL0)
+    at(12, sib_wait, 3, 0)
+    at(12, split_a, 3, 0)
+    at(13, c_send, 3, 0, ALL1)
+    for q in (0, 1):
+        at(13, z_wait, 4, q, q)
+        at(13, sib_send, 4, q)
+    at(14, c_send, 4, 1, ALL1)
+    at(14, own_o.wait)
+    for q in (0, 1):
+        at(14, sib_wait, 4, q)
+    at(14, split_a, 4, 0)
+    at(15, c_send, 4, 0, ALL1)
 
     @pl.loop(0, len(ORDER))
     def _(j):
@@ -463,7 +461,7 @@
             dma((9,)), dma((28,)), dma((3,)), dma((18,)), dma((18,)), dma((2,)), dma((30,)), dma((2,)), dma, dma,
         ],
         compiler_params=pltpu.CompilerParams(
-            collective_id=0, has_side_effects=True, vmem_limit_bytes=62 << 20
+            collective_id=0, has_side_effects=True, vmem_limit_bytes=213 << 18
         ),
         cost_estimate=pl.CostEstimate(flops=6442450944, bytes_accessed=4 << 20, transcendentals=0),
     )(a, b, other_terms, *small)

time: 66.6 us -> 62.9 us (0.944)
  Pallas kernels: 64.6 us -> 61.2 us
    pallas_call x1, Pallas kernels: 64.6 us -> 61.2 us  [local(): pl.pallas_call(kernel, out_shape=jax.ShapeDtypeStruct((512, 256), F32), i...]
    unnamed x1 -> x13, local copies, waits for them, and re-layouts: 1.87 us -> 1.52 us
where the time goes in v4:
time: 62.9 us; the launch traced here: 62.8 us
  Pallas kernels  61.2 us (97%)
  local copies, waits for them, and re-layouts  1.52 us (2%)
    pallas_call x1, Pallas kernels, local(): pl.pallas_call(kernel, out_shape=jax.ShapeDtypeStruct((512, 256), F32), i...  61.2 us
    unnamed x13, local copies, waits for them, and re-layouts  1.52 us

profile of v4, /device:TPU:1, one launch (start us, length us, event | category | flops | bytes accessed | tf_op | source)
XLA Modules:
  0.0 62.8 jit_solution(4547132143247121647)
XLA Ops:
  0.0 0.0 copy-start.4
  0.0 0.0 copy-start.5
  0.0 0.0 copy-start.2
  0.0 0.0 copy-start
  0.0 0.0 copy-start.1
  0.0 0.0 copy-start.3
  0.0 0.6 %copy-done.4 = s32[256]{0:T(256)S(1)} copy-done((s32[256]{0:T(256)S(1)}, s32[256]{0:T(256)}, u32[]{:S(2)}) %copy-start.4) | copy-done | bytes 1048
  0.7 0.0 copy-done.5
  0.7 0.0 copy-done.2
  0.7 0.0 copy-done
  0.7 0.0 copy-done.1
  0.7 0.0 copy-done.3
  0.8 61.2 %shard_map.91 = f32[512,256]{1,0:T(8,128)S(1)} custom-call(f32[2,2,16,2,8,128]{5,4,3,2,1,0:T(8,128)} %bitcast.17, f32[4,2,128,256]{3,2,1,0:T(8,128)} %bitcast.16, f32[512,256]{1,0:T(8,128)} %other_ref.1, s32[1,512]{1,0:T(1,128)S(1)} %bitcast.11, s32[1,512]{1,0:T(1,128)S(1)} %bitcast.12, s32[1,256]{1,0:T(1,128)S(1)} %bitcast.13, s32[1,256]{1,0:T(1,128)S(1)} %bitcast.14, ...), custom_call_target="tpu_custom_call" | custom-call | flops 6442450944 | bytes 4194304 | tf_op jit(solution)/shard_map/pallas_call | solution.py:442
  62.0 0.8 %copy.11 = f32[512,256]{1,0:T(8,128)} copy(f32[512,256]{1,0:T(8,128)S(1)} %shard_map.91) | data formatting | bytes 1048576
Async XLA Ops:
  0.0 0.7 %copy-start.4 = (s32[256]{0:T(256)S(1)}, s32[256]{0:T(256)}, u32[]{:S(2)}) copy-start(s32[256]{0:T(256)} %param.15) | copy-start | bytes 3076
  0.0 0.7 %copy-start.5 = (f32[100]{0:T(128)S(1)}, f32[100]{0:T(128)}, u32[]{:S(2)}) copy-start(f32[100]{0:T(128)} %param.16) | copy-start | bytes 1204
  0.0 0.7 %copy-start.2 = (s32[512]{0:T(512)S(1)}, s32[512]{0:T(512)}, u32[]{:S(2)}) copy-start(s32[512]{0:T(512)} %param.13) | copy-start | bytes 6148
  0.0 0.7 %copy-start = (f32[600]{0:T(1024)S(1)}, f32[600]{0:T(1024)}, u32[]{:S(2)}) copy-start(f32[600]{0:T(1024)} %refs_5_.1) | copy-start | bytes 7204
  0.0 0.7 %copy-start.1 = (s32[512]{0:T(512)S(1)}, s32[512]{0:T(512)}, u32[]{:S(2)}) copy-start(s32[512]{0:T(512)} %param.12) | copy-start | bytes 6148
  0.0 0.7 %copy-start.3 = (s32[256]{0:T(256)S(1)}, s32[256]{0:T(256)}, u32[]{:S(2)}) copy-start(s32[256]{0:T(256)} %param.14) | copy-start | bytes 3076

commit v5 on v4

--- a/solution.py
+++ b/solution.py
@@ -10,9 +10,10 @@
 START = (0, 64, 192, 320, 448, 512)
 CHUNKS = ((0, 0, 256), (1, 0, 128), (1, 128, 128), (1, 0, 256))
 ALL0, LOW1, HIGH1, ALL1 = range(4)
+ROWS = (64, 128, 256, 384)
 ORDER = (
-    (0, 1, ALL0), (2, 2, ALL0), (2, 2, LOW1), (0, 1, LOW1), (6, 2, ALL0), (6, 2, LOW1), (12, 1, ALL0),
-    (2, 2, HIGH1), (6, 2, HIGH1), (0, 1, HIGH1), (12, 1, ALL1), (15, 0, ALL0), (10, 1, ALL1), (15, 0, ALL1),
+    (0, 3, ALL0), (8, 1, ALL0), (0, 3, LOW1), (6, 2, LOW1), (6, 1, ALL0), (12, 1, ALL0),
+    (0, 3, HIGH1), (6, 2, HIGH1), (12, 1, ALL1), (15, 0, ALL0), (10, 1, ALL1), (15, 0, ALL1),
     (14, 0, ALL1), (10, 1, ALL0), (14, 0, ALL0),
 )
 
@@ -80,7 +81,13 @@
         remote(at, at, recv, sib).wait_recv()
 
     def z_sem(s, q, d):
-        return zr.at[(s - 1) * 8 + d * 4 + q if s < 4 else 24 + q]
+        if s == 1:
+            return zr.at[2 * q + d]
+        if s == 4:
+            return zr.at[8 + q // 2]
+        if q > 1:
+            return zr.at[6 + 4 * (s - 2) + 2 * q + d]
+        return zr.at[18 if s == 2 else 19 + (q + d) % 2]
 
     def z_send(s, q, d):
         def make():
@@ -90,12 +97,13 @@
 
         go(make)
 
-    def z_wait(s, q, d):
-        arrive(abuf.at[zof(s, d), xi[q], c], z_sem(s, q, d))
+    def z_pair(s, q, d):
+        at = abuf.at[zof(s, d), pl.ds(0, 2)] if s == 2 else abuf.at[zof(s, d), xi[q]]
+        arrive(at, z_sem(s, q, d))
 
     def z_step(s, q):
         for d in (q % 2, 1 - q % 2):
-            z_wait(s, q, d)
+            arrive(abuf.at[zof(s, d), xi[q], c], z_sem(s, q, d))
             if s < 3 or d == q % 2:
                 z_send(s, q, d)
 
@@ -108,23 +116,30 @@
             z_send(0, q, d)
 
     def sib_at(s, p, k, core):
-        if s == 4:
-            return abuf.at[zof(s, 0), xi[k], core], sr.at[14 + k]
-        where = abuf.at[zof(s, p), pl.ds(2 * (xh if k == 0 else 1 - xh), 2), core]
-        return where, sr.at[2 * (0 if s == 0 else 2 * s - 1 + p) + k]
+        pair = pl.ds(2 * (xh if k == 0 else 1 - xh), 2)
+        return abuf.at[zof(s, p), pair if s else slice(None), core]
+
+    def sib_sem(s, k):
+        return sr.at[0 if s == 0 else 2 * s - 1 + k]
 
     def sib_send(s, k):
         for p in sides(s):
 
             def make(p=p):
-                where, sem = sib_at(s, p, k, c)
-                return remote(where, where, sem, sib)
+                where = sib_at(s, p, k, c)
+                return remote(where, where, sib_sem(s, k), sib)
 
             go(make)
 
+    def sib_quarter(q):
+        def make():
+            where = abuf.at[zof(4, 0), xi[q], c]
+            return remote(where, where, sib_sem(4, q // 2), sib)
+
+        go(make)
+
     def sib_wait(s, k):
-        for p in sides(s):
-            arrive(*sib_at(s, p, k, 1 - c))
+        arrive(abuf.at[zof(s, 0), :, 1 - c] if s < 4 else sib_at(s, 0, k, 1 - c), sib_sem(s, k))
 
     def b_at(n, yy, groups=slice(None)):
         h, l0, nl = CHUNKS[n]
@@ -139,26 +154,24 @@
 
             def make(d=d):
                 src = b_ref.at[part(i, d), xl, :, l0 : l0 + nl] if h == 0 else b_at(n, y, part(i, d))
-                return remote(src, b_at(n, y, part(i, d)), yr.at[n * 6 + i * 2 + d], ydev[d])
+                return remote(src, b_at(n, y, part(i, d)), yr.at[n * 3 + i], ydev[d])
 
             go(make)
 
     def y_wait(n, i):
-        for d in range(2):
-            arrive(b_at(n, (ym, yp)[d], part(i, d)), yr.at[n * 6 + i * 2 + d])
+        arrive(b_at(n, ym), yr.at[n * 3 + i])
 
     def y_forward(n):
         for d in range(2):
 
             def make(d=d):
                 at = b_at(n, (ym, yp)[d], part(0, d))
-                return remote(at, at, yr.at[n * 6 + 4 + d], ydev[d])
+                return remote(at, at, yr.at[n * 3 + 2], ydev[d])
 
             go(make)
 
     def y_far(n):
-        for d in range(2):
-            arrive(b_at(n, y2, part(0, d)), yr.at[n * 6 + 4 + d])
+        arrive(b_at(n, y2), yr.at[n * 3 + 2])
 
     def e_send(n):
         h, l0, nl = CHUNKS[n]
@@ -203,29 +216,33 @@
         r0 = pl.multiple_of(first * 64, 64)
 
         def product(size):
-            rows = pl.ds(r0, size)
+            rows = pl.ds(pl.multiple_of(first // 2 * 128, 128), size)
             total = (
                 jnp.dot(alo[rows, :], bhi[h], preferred_element_type=F32)
                 + jnp.dot(ahi[rows, :], blo[h], preferred_element_type=F32)
                 + jnp.dot(ahi[rows, :], bhi[h], preferred_element_type=F32)
             )
-
-            @pl.when(low)
-            def _():
-                cbuf[h, rows, :128] = total[:, :128]
-
-            @pl.when(high)
-            def _():
-                cbuf[h, rows, 128:] = total[:, 128:]
-
-        for k in range(3):
-            pl.when(scale == k)(lambda k=k: product(64 << k))
+            for r in range(0, size, 64):
+                keep = (scale > 0) | (first % 2 == r // 64)
+                here = pl.ds(pl.multiple_of(first // 2 * 128 + r, 64), 64)
+
+                @pl.when(low & keep)
+                def _():
+                    cbuf[h, here, :128] = total[r : r + 64, :128]
+
+                @pl.when(high & keep)
+                def _():
+                    cbuf[h, here, 128:] = total[r : r + 64, 128:]
+
+        pl.when(scale < 2)(lambda: product(128))
+        pl.when(scale == 2)(lambda: product(256))
+        pl.when(scale == 3)(lambda: product(384))
 
         @pl.when((panel_h == h) & ((low & (xl == 0)) | (high & (xl == 1))))
         def _():
             lanes = pl.ds(pl.multiple_of(xl * 128, 128), 128)
 
-            @pl.loop(0, 2 + 2 * scale + 2 * (scale // 2))
+            @pl.loop(0, 2 * (1 + scale + scale // 2 + scale // 3))
             def _(i):
                 bb, g = (2 * first + i) // 4, (2 * first + i) % 4
                 s, both = (bb + 1) // 2, ((bb == 0) | (bb == 7)).astype(jnp.int32)
@@ -243,18 +260,13 @@
         size, lanes = START[s + 1] - START[s], slice(l0, l0 + nl)
         src = cbuf.at[h, rows_at(s, 0, k) : rows_at(s, 0, k) + size, lanes]
         dst = rbuf.at[q - 1, START[s] : START[s] + size, lanes]
-        return remote(src, dst, cr.at[s * 6 + 2 * (q - 1) + (1 if l0 else 0)], xdev[q])
-
-    c_sent = []
+        return remote(src, dst, cr.at[s], xdev[q])
 
     def c_send(*what):
         go(lambda: c_copy(*what))
-        c_sent.append(what)
 
     def finish(s):
-        for what in c_sent:
-            if what[0] == s:
-                c_copy(*what).wait_recv()
+        arrive(rbuf.at[:, START[s] : START[s + 1]], cr.at[s])
         for p in sides(s):
             zz = zof(s, p)
             for l in range(2):
@@ -284,15 +296,14 @@
     e_send(HIGH1)
     z_step(1, 0)
     x_step(2)
-    x_step(1)
     y_wait(ALL0, 0)
     y_forward(ALL0)
     own_b.wait()
     split_b(ALL0, y)
     x_step(3)
+    x_step(1)
     own_a.wait()
     sib_send(0, 0)
-    sib_send(0, 1)
     z_step(1, 2)
     e_wait(LOW1)
     y_send(LOW1, 0)
@@ -304,14 +315,16 @@
     y_wait(ALL0, 1)
     split_b(ALL0, ym)
     split_b(ALL0, yp)
-    z_step(1, 1)
+    z_step(1, 3)
+    sib_send(1, 1)
+    sib_wait(0, 0)
     for k in range(2):
-        sib_wait(0, k)
         split_a(0, k)
     split_b(LOW1, y)
-    z_step(1, 3)
-    sib_send(1, 1)
+    z_step(1, 1)
     sib_send(1, 0)
+    sib_wait(1, 1)
+    split_a(1, 1)
     y_far(ALL0)
     split_b(ALL0, y2)
     z_step(2, 2)
@@ -321,23 +334,23 @@
     def at(j, f, *a):
         before[j].append(lambda: f(*a))
 
+    at(0, sib_wait, 1, 0)
+    at(0, split_a, 1, 0)
     at(1, c_send, 0, 1, ALL0)
-    at(1, sib_wait, 1, 1)
-    at(1, split_a, 1, 1)
-    at(1, sib_wait, 1, 0)
-    at(1, split_a, 1, 0)
+    at(1, c_send, 1, 1, ALL0)
     at(1, y_wait, LOW1, 0)
     at(1, y_forward, LOW1)
     at(1, e_wait, HIGH1)
     at(1, y_send, HIGH1, 0)
     at(1, y_send, HIGH1, 1)
     at(1, split_b, HIGH1, y)
-    at(2, c_send, 1, 1, ALL0)
-    at(2, z_step, 2, 3)
-    at(2, sib_send, 2, 1)
+    at(1, z_step, 2, 3)
+    at(1, sib_send, 2, 1)
+    at(1, sib_wait, 2, 1)
+    at(1, split_a, 2, 1)
+    at(2, c_send, 2, 1, ALL0)
+    at(2, z_pair, 2, 0, 0)
     for q in (0, 1):
-        for d in (0, 1):
-            at(2, z_wait, 2, q, d)
         at(2, z_send, 2, q, q)
     at(2, sib_send, 2, 0)
     at(2, y_wait, LOW1, 1)
@@ -345,64 +358,58 @@
     at(2, split_b, LOW1, yp)
     at(2, y_far, LOW1)
     at(2, split_b, LOW1, y2)
+    at(3, c_send, 0, 0, LOW1)
+    at(3, c_send, 0, 1, LOW1)
     at(3, c_send, 1, 0, LOW1)
     at(3, c_send, 1, 1, LOW1)
-    at(4, c_send, 0, 0, LOW1)
-    at(4, c_send, 0, 1, LOW1)
-    at(4, z_step, 3, 2)
-    at(4, sib_wait, 2, 1)
-    at(4, split_a, 2, 1)
-    at(4, sib_wait, 2, 0)
-    at(4, split_a, 2, 0)
-    at(5, c_send, 2, 1, ALL0)
-    at(5, y_wait, HIGH1, 0)
-    at(5, y_forward, HIGH1)
-    at(6, c_send, 2, 0, LOW1)
-    at(6, c_send, 2, 1, LOW1)
-    at(6, z_step, 3, 3)
+    at(3, z_step, 3, 2)
+    at(3, sib_wait, 2, 0)
+    at(3, split_a, 2, 0)
+    at(4, c_send, 2, 0, LOW1)
+    at(4, c_send, 2, 1, LOW1)
+    at(4, y_wait, HIGH1, 0)
+    at(4, y_forward, HIGH1)
+    at(5, z_step, 3, 3)
     for q in (0, 1):
-        at(6, z_send, 2, q, 1 - q)
-    at(6, sib_send, 3, 1)
-    at(6, sib_wait, 3, 1)
-    at(6, split_a, 3, 1)
-    at(7, c_send, 3, 1, ALL0)
+        at(5, z_send, 2, q, 1 - q)
+    at(5, sib_send, 3, 1)
+    at(5, sib_wait, 3, 1)
+    at(5, split_a, 3, 1)
+    at(6, c_send, 3, 1, ALL0)
+    at(6, z_pair, 3, 0, 0)
     for q in (0, 1):
-        at(7, z_wait, 3, q, q)
-        at(7, z_send, 3, q, q)
-    at(7, y_wait, HIGH1, 1)
-    at(7, split_b, HIGH1, ym)
-    at(7, split_b, HIGH1, yp)
-    at(7, y_far, HIGH1)
-    at(7, split_b, HIGH1, y2)
-    at(8, c_send, 1, 0, HIGH1)
-    at(8, c_send, 1, 1, HIGH1)
+        at(6, z_send, 3, q, q)
+    at(6, y_wait, HIGH1, 1)
+    at(6, split_b, HIGH1, ym)
+    at(6, split_b, HIGH1, yp)
+    at(6, y_far, HIGH1)
+    at(6, split_b, HIGH1, y2)
+    at(7, c_send, 1, 0, HIGH1)
+    at(7, c_send, 1, 1, HIGH1)
+    at(7, c_send, 0, 0, HIGH1)
+    at(7, c_send, 0, 1, HIGH1)
+    at(7, z_pair, 4, 2, 0)
     for q in (2, 3):
-        at(8, z_wait, 4, q, q % 2)
-        at(8, sib_send, 4, q)
-    at(9, c_send, 2, 0, HIGH1)
-    at(9, c_send, 2, 1, HIGH1)
-    at(10, c_send, 0, 0, HIGH1)
-    at(10, c_send, 0, 1, HIGH1)
+        at(7, sib_quarter, q)
+    at(8, c_send, 2, 0, HIGH1)
+    at(8, c_send, 2, 1, HIGH1)
+    at(8, z_pair, 3, 0, 1)
+    at(8, sib_send, 3, 0)
+    at(9, c_send, 3, 1, ALL1)
+    at(9, sib_wait, 4, 1)
+    at(9, split_a, 4, 1)
+    at(10, c_send, 4, 1, ALL0)
+    at(10, sib_wait, 3, 0)
+    at(10, split_a, 3, 0)
+    at(11, c_send, 3, 0, ALL1)
+    at(11, z_pair, 4, 0, 0)
     for q in (0, 1):
-        at(10, z_wait, 3, q, 1 - q)
-    at(10, sib_send, 3, 0)
-    at(11, c_send, 3, 1, ALL1)
-    for q in (2, 3):
-        at(11, sib_wait, 4, q)
-    at(11, split_a, 4, 1)
-    at(12, c_send, 4, 1, ALL0)
-    at(12, sib_wait, 3, 0)
-    at(12, split_a, 3, 0)
-    at(13, c_send, 3, 0, ALL1)
-    for q in (0, 1):
-        at(13, z_wait, 4, q, q)
-        at(13, sib_send, 4, q)
-    at(14, c_send, 4, 1, ALL1)
-    at(14, own_o.wait)
-    for q in (0, 1):
-        at(14, sib_wait, 4, q)
-    at(14, split_a, 4, 0)
-    at(15, c_send, 4, 0, ALL1)
+        at(11, sib_quarter, q)
+    at(12, c_send, 4, 1, ALL1)
+    at(12, own_o.wait)
+    at(12, sib_wait, 4, 0)
+    at(12, split_a, 4, 0)
+    at(13, c_send, 4, 0, ALL1)
 
     @pl.loop(0, len(ORDER))
     def _(j):
@@ -458,7 +465,7 @@
             pltpu.VMEM((2, 8, 256), F32),
             pltpu.VMEM((512, 256), F32),
             *[pltpu.VMEM(v.shape, v.dtype) for v in small],
-            dma((9,)), dma((28,)), dma((3,)), dma((18,)), dma((18,)), dma((2,)), dma((30,)), dma((2,)), dma, dma,
+            dma((9,)), dma((21,)), dma((3,)), dma((9,)), dma((9,)), dma((2,)), dma((5,)), dma((2,)), dma, dma,
         ],
         compiler_params=pltpu.CompilerParams(
             collective_id=0, has_side_effects=True, vmem_limit_bytes=213 << 18

time: 62.9 us -> 61.9 us (0.984)
  Pallas kernels: 61.2 us -> 60.2 us
    pallas_call x1, Pallas kernels: 61.2 us -> 60.2 us  [local(): pl.pallas_call(kernel, out_shape=jax.ShapeDtypeStruct((512, 256), F32), i...]
where the time goes in v5:
time: 61.9 us; the launch traced here: 61.8 us
  Pallas kernels  60.2 us (97%)
  local copies, waits for them, and re-layouts  1.52 us (2%)
    pallas_call x1, Pallas kernels, local(): pl.pallas_call(kernel, out_shape=jax.ShapeDtypeStruct((512, 256), F32), i...  60.2 us
    unnamed x13, local copies, waits for them, and re-layouts  1.52 us

profile of v5, /device:TPU:1, one launch (start us, length us, event | category | flops | bytes accessed | tf_op | source)
XLA Modules:
  0.0 61.8 jit_solution(353369307259174345)
XLA Ops:
  0.0 0.0 copy-start.4
  0.0 0.0 copy-start.5
  0.0 0.0 copy-start.2
  0.0 0.0 copy-start
  0.0 0.0 copy-start.1
  0.0 0.0 copy-start.3
  0.0 0.6 %copy-done.4 = s32[256]{0:T(256)S(1)} copy-done((s32[256]{0:T(256)S(1)}, s32[256]{0:T(256)}, u32[]{:S(2)}) %copy-start.4) | copy-done | bytes 1048
  0.7 0.0 copy-done.5
  0.7 0.0 copy-done.2
  0.7 0.0 copy-done
  0.7 0.0 copy-done.1
  0.7 0.0 copy-done.3
  0.8 60.2 %shard_map.91 = f32[512,256]{1,0:T(8,128)S(1)} custom-call(f32[2,2,16,2,8,128]{5,4,3,2,1,0:T(8,128)} %bitcast.17, f32[4,2,128,256]{3,2,1,0:T(8,128)} %bitcast.16, f32[512,256]{1,0:T(8,128)} %other_ref.1, s32[1,512]{1,0:T(1,128)S(1)} %bitcast.11, s32[1,512]{1,0:T(1,128)S(1)} %bitcast.12, s32[1,256]{1,0:T(1,128)S(1)} %bitcast.13, s32[1,256]{1,0:T(1,128)S(1)} %bitcast.14, ...), custom_call_target="tpu_custom_call" | custom-call | flops 6442450944 | bytes 4194304 | tf_op jit(solution)/shard_map/pallas_call | solution.py:449
  61.0 0.8 %copy.11 = f32[512,256]{1,0:T(8,128)} copy(f32[512,256]{1,0:T(8,128)S(1)} %shard_map.91) | data formatting | bytes 1048576
Async XLA Ops:
  0.0 0.7 %copy-start.4 = (s32[256]{0:T(256)S(1)}, s32[256]{0:T(256)}, u32[]{:S(2)}) copy-start(s32[256]{0:T(256)} %param.15) | copy-start | bytes 3076
  0.0 0.7 %copy-start.5 = (f32[100]{0:T(128)S(1)}, f32[100]{0:T(128)}, u32[]{:S(2)}) copy-start(f32[100]{0:T(128)} %param.16) | copy-start | bytes 1204
  0.0 0.7 %copy-start.2 = (s32[512]{0:T(512)S(1)}, s32[512]{0:T(512)}, u32[]{:S(2)}) copy-start(s32[512]{0:T(512)} %param.13) | copy-start | bytes 6148
  0.0 0.7 %copy-start = (f32[600]{0:T(1024)S(1)}, f32[600]{0:T(1024)}, u32[]{:S(2)}) copy-start(f32[600]{0:T(1024)} %refs_5_.1) | copy-start | bytes 7204
  0.0 0.7 %copy-start.1 = (s32[512]{0:T(512)S(1)}, s32[512]{0:T(512)}, u32[]{:S(2)}) copy-start(s32[512]{0:T(512)} %param.12) | copy-start | bytes 6148
  0.0 0.7 %copy-start.3 = (s32[256]{0:T(256)S(1)}, s32[256]{0:T(256)}, u32[]{:S(2)}) copy-start(s32[256]{0:T(256)} %param.14) | copy-start | bytes 3076

commit v6 on v5

--- a/solution.py
+++ b/solution.py
@@ -369,10 +369,10 @@
     at(4, c_send, 2, 1, LOW1)
     at(4, y_wait, HIGH1, 0)
     at(4, y_forward, HIGH1)
-    at(5, z_step, 3, 3)
+    at(4, z_step, 3, 3)
     for q in (0, 1):
-        at(5, z_send, 2, q, 1 - q)
-    at(5, sib_send, 3, 1)
+        at(4, z_send, 2, q, 1 - q)
+    at(4, sib_send, 3, 1)
     at(5, sib_wait, 3, 1)
     at(5, split_a, 3, 1)
     at(6, c_send, 3, 1, ALL0)

time: 61.9 us -> 61 us (0.985)
  Pallas kernels: 60.2 us -> 59.4 us
    pallas_call x1, Pallas kernels: 60.2 us -> 59.4 us  [local(): pl.pallas_call(kernel, out_shape=jax.ShapeDtypeStruct((512, 256), F32), i...]
where the time goes in v6:
time: 61 us; the launch traced here: 60.9 us
  Pallas kernels  59.4 us (97%)
  local copies, waits for them, and re-layouts  1.52 us (2%)
    pallas_call x1, Pallas kernels, local(): pl.pallas_call(kernel, out_shape=jax.ShapeDtypeStruct((512, 256), F32), i...  59.4 us
    unnamed x13, local copies, waits for them, and re-layouts  1.52 us

profile of v6, /device:TPU:1, one launch (start us, length us, event | category | flops | bytes accessed | tf_op | source)
XLA Modules:
  0.0 60.9 jit_solution(2370161604860029576)
XLA Ops:
  0.0 0.0 copy-start.4
  0.0 0.0 copy-start.5
  0.0 0.0 copy-start.2
  0.0 0.0 copy-start
  0.0 0.0 copy-start.1
  0.0 0.0 copy-start.3
  0.0 0.6 %copy-done.4 = s32[256]{0:T(256)S(1)} copy-done((s32[256]{0:T(256)S(1)}, s32[256]{0:T(256)}, u32[]{:S(2)}) %copy-start.4) | copy-done | bytes 1048
  0.7 0.0 copy-done.5
  0.7 0.0 copy-done.2
  0.7 0.0 copy-done
  0.7 0.0 copy-done.1
  0.7 0.0 copy-done.3
  0.8 59.4 %shard_map.91 = f32[512,256]{1,0:T(8,128)S(1)} custom-call(f32[2,2,16,2,8,128]{5,4,3,2,1,0:T(8,128)} %bitcast.17, f32[4,2,128,256]{3,2,1,0:T(8,128)} %bitcast.16, f32[512,256]{1,0:T(8,128)} %other_ref.1, s32[1,512]{1,0:T(1,128)S(1)} %bitcast.11, s32[1,512]{1,0:T(1,128)S(1)} %bitcast.12, s32[1,256]{1,0:T(1,128)S(1)} %bitcast.13, s32[1,256]{1,0:T(1,128)S(1)} %bitcast.14, ...), custom_call_target="tpu_custom_call" | custom-call | flops 6442450944 | bytes 4194304 | tf_op jit(solution)/shard_map/pallas_call | solution.py:449
  60.1 0.8 %copy.11 = f32[512,256]{1,0:T(8,128)} copy(f32[512,256]{1,0:T(8,128)S(1)} %shard_map.91) | data formatting | bytes 1048576
Async XLA Ops:
  0.0 0.7 %copy-start.4 = (s32[256]{0:T(256)S(1)}, s32[256]{0:T(256)}, u32[]{:S(2)}) copy-start(s32[256]{0:T(256)} %param.15) | copy-start | bytes 3076
  0.0 0.7 %copy-start.5 = (f32[100]{0:T(128)S(1)}, f32[100]{0:T(128)}, u32[]{:S(2)}) copy-start(f32[100]{0:T(128)} %param.16) | copy-start | bytes 1204
  0.0 0.7 %copy-start.2 = (s32[512]{0:T(512)S(1)}, s32[512]{0:T(512)}, u32[]{:S(2)}) copy-start(s32[512]{0:T(512)} %param.13) | copy-start | bytes 6148
  0.0 0.7 %copy-start = (f32[600]{0:T(1024)S(1)}, f32[600]{0:T(1024)}, u32[]{:S(2)}) copy-start(f32[600]{0:T(1024)} %refs_5_.1) | copy-start | bytes 7204
  0.0 0.7 %copy-start.1 = (s32[512]{0:T(512)S(1)}, s32[512]{0:T(512)}, u32[]{:S(2)}) copy-start(s32[512]{0:T(512)} %param.12) | copy-start | bytes 6148
  0.0 0.7 %copy-start.3 = (s32[256]{0:T(256)S(1)}, s32[256]{0:T(256)}, u32[]{:S(2)}) copy-start(s32[256]{0:T(256)} %param.14) | copy-start | bytes 3076

commit v7 on v6

--- a/solution.py
+++ b/solution.py
@@ -184,7 +184,7 @@
         h, l0, nl = CHUNKS[n]
         lanes = slice(l0, l0 + nl)
 
-        @pl.loop(0, 16)
+        @pl.loop(0, 16, unroll=2)
         def _(i):
             g, r = i // 4, pl.multiple_of((i % 4) * 32, 32)
             v = bbuf[h, yy, g, pl.ds(r, 32), lanes]
@@ -197,7 +197,7 @@
         return (64 * k if s in (0, 4) else 128 * k - 128) + 256 * s - (128 if s == 4 else 0) + 64 * p
 
     def split_a(s, k):
-        @pl.loop(0, 16)
+        @pl.loop(0, 16, unroll=2)
         def _(j):
             lanes = pl.ds(pl.multiple_of(j * 128, 128), 128)
             for p in sides(s):
@@ -336,26 +336,26 @@
 
     at(0, sib_wait, 1, 0)
     at(0, split_a, 1, 0)
+    at(0, y_wait, LOW1, 0)
+    at(0, y_forward, LOW1)
+    at(0, e_wait, HIGH1)
+    at(0, y_send, HIGH1, 0)
+    at(0, y_send, HIGH1, 1)
     at(1, c_send, 0, 1, ALL0)
     at(1, c_send, 1, 1, ALL0)
-    at(1, y_wait, LOW1, 0)
-    at(1, y_forward, LOW1)
-    at(1, e_wait, HIGH1)
-    at(1, y_send, HIGH1, 0)
-    at(1, y_send, HIGH1, 1)
     at(1, split_b, HIGH1, y)
     at(1, z_step, 2, 3)
     at(1, sib_send, 2, 1)
     at(1, sib_wait, 2, 1)
     at(1, split_a, 2, 1)
     at(2, c_send, 2, 1, ALL0)
+    at(2, y_wait, LOW1, 1)
+    at(2, split_b, LOW1, ym)
+    at(2, split_b, LOW1, yp)
     at(2, z_pair, 2, 0, 0)
     for q in (0, 1):
         at(2, z_send, 2, q, q)
     at(2, sib_send, 2, 0)
-    at(2, y_wait, LOW1, 1)
-    at(2, split_b, LOW1, ym)
-    at(2, split_b, LOW1, yp)
     at(2, y_far, LOW1)
     at(2, split_b, LOW1, y2)
     at(3, c_send, 0, 0, LOW1)
@@ -401,10 +401,10 @@
     at(10, c_send, 4, 1, ALL0)
     at(10, sib_wait, 3, 0)
     at(10, split_a, 3, 0)
+    at(10, z_pair, 4, 0, 0)
+    for q in (0, 1):
+        at(10, sib_quarter, q)
     at(11, c_send, 3, 0, ALL1)
-    at(11, z_pair, 4, 0, 0)
-    for q in (0, 1):
-        at(11, sib_quarter, q)
     at(12, c_send, 4, 1, ALL1)
     at(12, own_o.wait)
     at(12, sib_wait, 4, 0)

time: 61 us -> 60.6 us (level)
  no operation moved by 1% of the time
where the time goes in v7:
time: 60.6 us; the launch traced here: 60.5 us
  Pallas kernels  59 us (97%)
  local copies, waits for them, and re-layouts  1.52 us (3%)
    pallas_call x1, Pallas kernels, local(): pl.pallas_call(kernel, out_shape=jax.ShapeDtypeStruct((512, 256), F32), i...  59 us
    unnamed x13, local copies, waits for them, and re-layouts  1.52 us

profile of v7, /device:TPU:1, one launch (start us, length us, event | category | flops | bytes accessed | tf_op | source)
XLA Modules:
  0.0 60.5 jit_solution(6409051654409867405)
XLA Ops:
  0.0 0.0 copy-start.4
  0.0 0.0 copy-start.5
  0.0 0.0 copy-start.2
  0.0 0.0 copy-start
  0.0 0.0 copy-start.1
  0.0 0.0 copy-start.3
  0.0 0.6 %copy-done.4 = s32[256]{0:T(256)S(1)} copy-done((s32[256]{0:T(256)S(1)}, s32[256]{0:T(256)}, u32[]{:S(2)}) %copy-start.4) | copy-done | bytes 1048
  0.7 0.0 copy-done.5
  0.7 0.0 copy-done.2
  0.7 0.0 copy-done
  0.7 0.0 copy-done.1
  0.7 0.0 copy-done.3
  0.8 59.0 %shard_map.91 = f32[512,256]{1,0:T(8,128)S(1)} custom-call(f32[2,2,16,2,8,128]{5,4,3,2,1,0:T(8,128)} %bitcast.17, f32[4,2,128,256]{3,2,1,0:T(8,128)} %bitcast.16, f32[512,256]{1,0:T(8,128)} %other_ref.1, s32[1,512]{1,0:T(1,128)S(1)} %bitcast.11, s32[1,512]{1,0:T(1,128)S(1)} %bitcast.12, s32[1,256]{1,0:T(1,128)S(1)} %bitcast.13, s32[1,256]{1,0:T(1,128)S(1)} %bitcast.14, ...), custom_call_target="tpu_custom_call" | custom-call | flops 6442450944 | bytes 4194304 | tf_op jit(solution)/shard_map/pallas_call | solution.py:449
  59.7 0.8 %copy.11 = f32[512,256]{1,0:T(8,128)} copy(f32[512,256]{1,0:T(8,128)S(1)} %shard_map.91) | data formatting | bytes 1048576
Async XLA Ops:
  0.0 0.7 %copy-start.4 = (s32[256]{0:T(256)S(1)}, s32[256]{0:T(256)}, u32[]{:S(2)}) copy-start(s32[256]{0:T(256)} %param.15) | copy-start | bytes 3076
  0.0 0.7 %copy-start.5 = (f32[100]{0:T(128)S(1)}, f32[100]{0:T(128)}, u32[]{:S(2)}) copy-start(f32[100]{0:T(128)} %param.16) | copy-start | bytes 1204
  0.0 0.7 %copy-start.2 = (s32[512]{0:T(512)S(1)}, s32[512]{0:T(512)}, u32[]{:S(2)}) copy-start(s32[512]{0:T(512)} %param.13) | copy-start | bytes 6148
  0.0 0.7 %copy-start = (f32[600]{0:T(1024)S(1)}, f32[600]{0:T(1024)}, u32[]{:S(2)}) copy-start(f32[600]{0:T(1024)} %refs_5_.1) | copy-start | bytes 7204
  0.0 0.7 %copy-start.1 = (s32[512]{0:T(512)S(1)}, s32[512]{0:T(512)}, u32[]{:S(2)}) copy-start(s32[512]{0:T(512)} %param.12) | copy-start | bytes 6148
  0.0 0.7 %copy-start.3 = (s32[256]{0:T(256)S(1)}, s32[256]{0:T(256)}, u32[]{:S(2)}) copy-start(s32[256]{0:T(256)} %param.14) | copy-start | bytes 3076
